TPU v7x, 128 devices: a whole 4x4x4 slice. The times are simulated.
128 devices in a mesh: rep: 16 (over y, x_hi, core), fsdp: 8 (over x_lo, z).
Axes of the slice: x: 4 (x_hi: 2, x_lo: 2; x = x_hi * 2 + x_lo), y: 4, z: 4, core: 2. Of those that a mesh axis runs over, the one named last changes fastest.
Arguments:
- momentum: float32 [16, 2560, 2560], P('rep', 'fsdp'), may hold values from -6 to 6
- gradient: bfloat16 [16, 2560, 2560], P('rep', 'fsdp'), may hold values from -6 to 6
- weights: bfloat16 [2560, 2560], P('fsdp'), may hold values from -0.125 to 0.125
- inputs: bfloat16 [16, 5120, 2560], P('rep', 'fsdp'), may hold values from -6 to 6
Outputs:
- new_momentum: float32 [16, 2560, 2560], P('rep', 'fsdp')
- update: float32 [2560, 2560], P('fsdp')
- outputs: bfloat16 [16, 5120, 2560], P('rep', 'fsdp')
All inputs are finite; a program needn't handle non-finite values.
Results may differ from a plain program's by a relative error of at most 0.005.
Values may be sent and summed in bfloat16 or wider, within the bound.
No kernel may reach another device: no remote copies, remote signals or barrier semaphores. Data moves between devices by JAX's collectives and lax.ppermute only.
A program may use at most 192 MiB of HBM per device.

v0:
```python
import math

import jax
import jax.numpy as jnp
from jax import lax
from jax.sharding import PartitionSpec as P

decay = 0.9
step_size = 0.1
highest = lax.Precision.HIGHEST


def dct_basis():
    freq = jnp.arange(16).astype(jnp.float32)[:, None]
    place = jnp.arange(64).astype(jnp.float32)[None, :]
    table = jnp.cos(math.pi * (2.0 * place + 1.0) * freq / 128.0) * math.sqrt(2.0 / 64.0)
    scale = jnp.where(jnp.arange(16)[:, None] == 0, math.sqrt(0.5), 1.0).astype(jnp.float32)
    return table * scale


def column_table(basis, col_count):
    blocks = col_count // 64
    repeated = jnp.tile(basis.T, (blocks, blocks))
    owner_col = jnp.arange(col_count) // 64
    owner_band = jnp.arange(blocks * 16) // 16
    same_block = owner_col[:, None] == owner_band[None, :]
    return jnp.where(same_block, repeated, jnp.zeros_like(repeated))


def band_of(field, basis, columns):
    row_count = field.shape[0]
    right_side = jnp.dot(field, columns, precision=highest, preferred_element_type=jnp.float32)
    right_side = right_side.reshape(row_count // 64, 64, right_side.shape[1])
    return jnp.einsum("in,anw->aiw", basis, right_side, precision=highest)


def left_inverse(band, basis):
    blocks = jnp.einsum("in,aiw->anw", basis, band, precision=highest)
    return blocks.reshape(band.shape[0] * 64, band.shape[2])


def right_inverse(partial_value, columns):
    return jnp.dot(partial_value, columns.T, precision=highest, preferred_element_type=jnp.float32)


def shards(momentum, gradient, weights, inputs):
    basis = dct_basis()
    columns = column_table(basis, momentum.shape[2])
    moment = decay * momentum[0] + gradient[0].astype(jnp.float32)
    coeffs = band_of(moment, basis, columns)
    new_momentum = (moment - right_inverse(left_inverse(coeffs, basis), columns))[None]
    mean_band = lax.psum(coeffs, "rep") / lax.axis_size("rep")
    partial_value = left_inverse(mean_band, basis)
    update = right_inverse(partial_value, columns)
    tokens = inputs[0]
    new_weights = (weights.astype(jnp.float32) - step_size * update).astype(jnp.bfloat16)
    result = jnp.dot(
        tokens,
        lax.all_gather(new_weights, "fsdp", axis=0, tiled=True),
        preferred_element_type=jnp.float32,
    )
    return (new_momentum, update, result.astype(jnp.bfloat16)[None])


def solution(mesh):
    placed = (
        P("rep", "fsdp", None),
        P("rep", "fsdp", None),
        P("fsdp", None),
        P("rep", "fsdp", None),
    )
    return jax.shard_map(
        shards,
        mesh=mesh,
        in_specs=placed,
        out_specs=(P("rep", "fsdp", None), P("fsdp", None), P("rep", "fsdp", None)),
        check_vma=False,
    )
```

profile of v0, /device:TPU:1, one launch (start us, length us, event | category | flops | bytes accessed | tf_op | source)
XLA Modules:
  0.0 356.8 jit_solution(12191046332914206584)
XLA Ops:
  7.2 0.0 copy-start
  7.3 0.1 cosine_multiply_fusion.4
  7.4 5.1 %compare_select_fusion = f32[40,64,40,16]{1,0,3,2:T(8,128)} fusion(f32[64,16]{0,1:T(8,128)S(1)} %cosine_multiply_fusion.4, s32[40,16]{1,0:T(8,128)S(1)} %add_select_fusion, s32[40,64]{1,0:T(8,128)S(1)} %add_select_fusion.1), kind=kLoop, calls=%fused_computation | loop fusion | flops 3276800 | bytes 6570496 | tf_op jit(solution)/shard_map/jit(_where)/select_n | solution.py:27
  12.5 11.7 %reshape.257 = f32[2560,640,1]{0,1,2:T(8,128)} reshape(f32[40,64,40,16]{1,0,3,2:T(8,128)} %compare_select_fusion) | data formatting | bytes 13107200 | tf_op jit(solution)/shard_map/jit(_where)/select_n | solution.py:27
  24.2 0.0 copy-start.2
  24.2 3.0 convert_add_fusion
  27.3 0.0 copy-start.1
  27.3 2.1 copy-done.2
  29.4 8.2 %fusion.29 = f32[5,64,640]{2,1,0:T(8,128)S(1)} fusion(f32[5,64,2560]{2,1,0:T(8,128)S(1)} %bitcast.44, f32[2560,640,1]{0,1,2:T(8,128)S(1)} %copy-done.2), kind=kOutput, calls=%fused_computation.48 | convolution fusion | flops 6291456000 | bytes 10649600 | tf_op jit(solution)/shard_map/dot_general | solution.py:32
  37.6 0.0 copy-done.1
  37.6 0.6 convolution_bitcast_fusion
  38.2 0.0 copy-start.3
  38.2 1.9 fusion.9
  40.1 0.0 all-reduce.2.cloned.1.call-start
  40.1 0.0 copy-done.3
  40.1 0.7 all-reduce.2.cloned.1.call-update
  40.8 0.2 all-gather.2.cloned.1.call-start
  41.0 11.7 %select_n.78 = f32[2560,640]{0,1:T(8,128)} reshape(f32[40,64,40,16]{1,0,3,2:T(8,128)} %compare_select_fusion) | data formatting | bytes 13107200 | tf_op jit(solution)/shard_map/jit(_where)/select_n | solution.py:27
  52.8 126.9 %all-reduce.2.cloned.1.call-done = f32[5,16,640]{2,1,0:T(8,128)} async-done(((f32[5,16,640]{2,1,0:T(8,128)}), f32[5,16,640]{2,1,0:T(8,128)}) %all-reduce.2.cloned.1.call-update) | async-done | bytes 204816 | tf_op jit(solution)/shard_map/psum | solution.py:52
  179.7 1.9 fusion.3
  181.6 12.0 %subtract_convert_fusion = (bf16[320,2560]{1,0:T(8,128)(2,1)}, f32[320,2560]{1,0:T(8,128)}) fusion(bf16[320,2560]{1,0:T(8,128)(2,1)} %param.6, f32[320,640]{1,0:T(8,128)S(1)} %bitcast.45, f32[2560,640]{0,1:T(8,128)} %select_n.78), kind=kOutput, calls=%fused_computation.6 | convolution fusion | flops 6294732800 | bytes 13926400 | tf_op jit(solution)/shard_map/dot_general | solution.py:43
  193.5 0.0 all-gather.2.cloned.1.call-update
  193.5 12.1 %fusion = f32[1,320,2560]{2,1,0:T(8,128)} fusion(f32[320,640]{1,0:T(8,128)} %bitcast.46, f32[2560,640]{0,1:T(8,128)} %select_n.78, f32[1,320,2560]{2,1,0:T(8,128)} %copy-done.1), kind=kOutput, calls=%fused_computation.3 | convolution fusion | flops 6292275200 | bytes 13926400 | tf_op jit(solution)/shard_map/dot_general | solution.py:43
  205.6 124.0 %all-gather.2.cloned.1.call-done = bf16[2560,2560]{1,0:T(8,128)(2,1)} async-done(((bf16[320,2560]{1,0:T(8,128)(2,1)}), bf16[2560,2560]{1,0:T(8,128)(2,1)}) %all-gather.2.cloned.1.call-update) | async-done | bytes 13107216 | tf_op jit(solution)/shard_map/all_gather | solution.py:59
  329.6 0.0 copy-done
  329.6 14.7 %fusion.1 = bf16[1,640,2560]{1,2,0:T(8,128)(2,1)} fusion(bf16[2560,2560]{1,0:T(8,128)(2,1)} %all-gather.2.cloned.1.call-done, bf16[1,640,2560]{2,1,0:T(8,128)(2,1)S(1)} %copy-done), kind=kOutput, calls=%fused_computation.4 | convolution fusion | flops 8390246400 | bytes 19660800 | tf_op jit(solution)/shard_map/dot_general | solution.py:57
  344.3 5.7 %copy.8 = bf16[1,640,2560]{2,1,0:T(8,128)(2,1)} copy(bf16[1,640,2560]{1,2,0:T(8,128)(2,1)} %fusion.1) | data formatting | bytes 6553600
  (5 shorter events, 0.0 us)
Async XLA Ops:
  7.2 322.5 %copy-start = (bf16[1,640,2560]{2,1,0:T(8,128)(2,1)S(1)}, bf16[1,640,2560]{2,1,0:T(8,128)(2,1)}, u32[]{:S(2)}) copy-start(bf16[1,640,2560]{2,1,0:T(8,128)(2,1)} %param.7) | copy-start | bytes 9830404
  24.2 5.1 %copy-start.2 = (f32[2560,640,1]{0,1,2:T(8,128)S(1)}, f32[2560,640,1]{0,1,2:T(8,128)}, u32[]{:S(2)}) copy-start(f32[2560,640,1]{0,1,2:T(8,128)} %reshape.257) | copy-start | bytes 19660804
  27.3 10.3 %copy-start.1 = (f32[1,320,2560]{2,1,0:T(8,128)}, f32[1,320,2560]{2,1,0:T(8,128)S(1)}, u32[]{:S(2)}) copy-start(f32[1,320,2560]{2,1,0:T(8,128)S(1)} %convert_add_fusion) | copy-start | bytes 9830404
  38.2 1.9 copy-start.3
  40.1 139.6 %all-reduce.2.cloned.1.call-start = ((), (), s32[]{:S(2)}) async-start(), calls=%async_computation | async-start | bytes 409600 | tf_op jit(solution)/shard_map/psum | solution.py:52
  40.8 288.8 %all-gather.2.cloned.1.call-start = ((), (), s32[]{:S(2)}) async-start(), calls=%async_computation.1 | async-start | bytes 14745600 | tf_op jit(solution)/shard_map/all_gather | solution.py:59
Sparse Core Ops, SparseCore 0:
  43.9 135.6 all-reduce.1
  193.7 135.9 all-gather.1
where the time goes:
time: 358 us; the launch traced here: 357 us
  waiting for transfers between devices  252 us (70%)
  matrix products  51.3 us (14%)
  local copies, waits for them, and re-layouts  31.3 us (9%)
  between operations  14.1 us (4%)
  other arithmetic  8.29 us (2%)
    psum x1, waiting for transfers between devices, shards(): mean_band = lax.psum(coeffs, 'rep') / lax.axis_size('rep')  127 us
    all_gather x1, waiting for transfers between devices, shards(): lax.all_gather(new_weights, 'fsdp', axis=0, tiled=True)  124 us
    dot_general x2, matrix products, right_inverse(): jnp.dot(partial_value, columns.T, precision=highest, preferred_element_ty...  24.1 us
    select_n x2, local copies, waits for them, and re-layouts, column_table(): return jnp.where(same_block, repeated, jnp.zeros_like(repeated))  23.5 us
    dot_general x1, matrix products, shards(): jnp.dot(tokens, lax.all_gather(new_weights, 'fsdp', axis=0, tiled=True),...  14.7 us
    dot_general x1, matrix products, band_of(): jnp.dot(field, columns, precision=highest, preferred_element_type=jnp.flo...  8.17 us
    unnamed x9, local copies, waits for them, and re-layouts  7.82 us
  transfers between devices with their start and end apart: 2, of which 2 were waited for; matrix products, arithmetic and copies ran while one was open for 7% of the time, Pallas kernels for 0%

commit v1 on v0

v1 whole, which is shorter than its diff:
```python
import functools
import math

import jax
import jax.numpy as jnp
import ml_dtypes
import numpy as np
from jax import lax
from jax.experimental import pallas as pl
from jax.experimental.pallas import tpu as pltpu
from jax.sharding import PartitionSpec as P

f32, bf16 = jnp.float32, jnp.bfloat16
BOTH = ("rep", "fsdp")
decay = 0.9
step_size = 0.1
ROWS, COLS, TOKENS = 320, 2560, 640
BANDS = 16 * COLS // 64
TILE_ROWS = 16 * ROWS // 64
HALF = BANDS // 2
WIDE = 512
NARROW = 128
N_REP = 16


def place_of(device):
    rep, shard = divmod(device, 8)
    return (rep // 2 % 2) * 2 + shard // 4, rep // 4, shard % 4, rep % 2


def device_at(x, y, z, core):
    x, y, z = x % 4, y % 4, z % 4
    return ((y * 2 + x // 2) * 2 + core % 2) * 8 + (x % 2) * 4 + z


def moved(value, first, second=None):
    pairs = []
    for device in range(128):
        x, y, z, core = place_of(device)
        dx, dy, dz, dc = first if second is None or core == 0 else second
        pairs.append((device, device_at(x + dx, y + dy, z + dz, core + dc)))
    return lax.ppermute(value, BOTH, pairs)


def along_z(value):
    return moved(value, (0, 0, 1, 0), (0, 0, -1, 0))


def along_x(value):
    return moved(value, (1, 0, 0, 0), (-1, 0, 0, 0))


def across(value):
    return moved(value, (0, 0, 0, 1))


def by(value, axis, distance):
    return moved(value, tuple(distance if k == axis else 0 for k in range(4)))


def basis_table():
    freq = np.arange(16)[:, None]
    spot = np.arange(64)[None, :]
    table = np.cos(math.pi * (2 * spot + 1) * freq / 128) * math.sqrt(2 / 64)
    table[0] = math.sqrt(1 / 64)
    return table


def halves(table):
    high = table.astype(ml_dtypes.bfloat16)
    low = (table - high.astype(np.float64)).astype(ml_dtypes.bfloat16)
    return high, low


def tables():
    basis = basis_table()
    left_high, left_low = halves(np.kron(np.eye(ROWS // 64), basis))
    right_high, right_low = halves(np.kron(np.eye(WIDE // 64), basis.T))
    step_high, step_low = halves(np.kron(np.eye(4), basis) * (-step_size / N_REP))
    return {
        "left": np.concatenate([left_high, left_low], 0),
        "right": np.stack([right_high, right_low]),
        "left_t": np.concatenate([left_high.T, left_high.T, left_low.T], 1),
        "right_t": np.concatenate([right_high.T, right_high.T, right_low.T], 0),
        "right_pair": np.concatenate([right_high, right_low], 1),
        "step": np.concatenate([step_high, step_high, step_low, step_low], 0),
    }


def dot(a, b):
    return jnp.dot(a, b, preferred_element_type=f32)


def split(value):
    high = value.astype(bf16)
    return high, (value - high.astype(f32)).astype(bf16)


def core_of():
    return lax.rem(lax.axis_index("rep"), 2)


def whole(shape):
    return pl.BlockSpec(shape, lambda j: (0,) * len(shape))


ANY = pl.BlockSpec(memory_space=pl.ANY)
VMEM = pl.BlockSpec(memory_space=pltpu.VMEM)


def params(megabytes):
    return pltpu.CompilerParams(vmem_limit_bytes=megabytes * 2**20)


def call(kernel, ins, outs, scratch=(), grid=(), megabytes=24, name=None, after=(), through=()):
    n_in, n_out, n_extra = len(ins), len(outs), len(after) + len(through)
    token = ((8, 128), f32, whole((8, 128)) if grid else VMEM)

    def body(*refs):
        n = n_in + n_extra
        token_ref = refs[n + n_out]
        token_ref[...] = jnp.zeros(token_ref.shape, f32)
        kernel(*refs[:n_in], *refs[n : n + n_out], *refs[n + n_out + 1 + len(through) :])

    return pl.pallas_call(
        body,
        grid=grid,
        out_shape=tuple(jax.ShapeDtypeStruct(shape, dtype) for shape, dtype, _ in (*outs, token))
        + tuple(jax.ShapeDtypeStruct(array.shape, array.dtype) for array in through),
        in_specs=[spec for _, spec in ins] + [ANY] * n_extra,
        out_specs=tuple(spec for _, _, spec in (*outs, token)) + (ANY,) * len(through),
        scratch_shapes=list(scratch),
        input_output_aliases={
            n_in + len(after) + k: n_out + 1 + k for k in range(len(through))
        },
        compiler_params=params(megabytes),
        cost_estimate=pl.CostEstimate(flops=1, transcendentals=0, bytes_accessed=1),
        name=name,
    )(*[array for array, _ in ins], *after, *through)


def column_block(rows, width):
    return pl.BlockSpec((rows, width), lambda j: (0, j))


def column_block_of_one(rows, width):
    return pl.BlockSpec((1, rows, width), lambda j: (0, 0, j))


N_WIDE = COLS // WIDE
HALF_ROWS = ROWS // 2
QUARTER = ROWS // 4


def band_kernel(
    m_ref, g_ref, w_ref, left_ref, right_ref,
    c_ref, mine_ref, theirs_ref, moment_ref, first_ref, second_ref,
    g_buffer, left, right, sems,
):
    core = core_of()

    def copies(j):
        columns = pl.ds(j * WIDE, WIDE)
        return (
            pltpu.make_async_copy(m_ref.at[0, :, columns], moment_ref.at[:, columns], sems.at[2 * j]),
            pltpu.make_async_copy(g_ref.at[0, :, columns], g_buffer.at[:, columns], sems.at[2 * j + 1]),
        )

    def rows(which):
        return w_ref.at[pl.ds(pl.multiple_of(which * HALF_ROWS, HALF_ROWS), HALF_ROWS)]

    base = 2 * N_WIDE
    others = (
        pltpu.make_async_copy(left_ref, left, sems.at[base]),
        pltpu.make_async_copy(right_ref, right, sems.at[base + 1]),
        pltpu.make_async_copy(rows(core), first_ref, sems.at[base + 2]),
        pltpu.make_async_copy(rows(1 - core), second_ref, sems.at[base + 3]),
    )
    for copy in (*others[:2], *copies(0), *copies(1), *copies(2), *copies(3), *copies(4), *others[2:]):
        copy.start()
    for copy in others[:2]:
        copy.wait()
    for j in range(N_WIDE):
        for copy in copies(j):
            copy.wait()
        columns = slice(j * WIDE, (j + 1) * WIDE)
        moment = decay * moment_ref[:, columns] + g_buffer[:, columns].astype(f32)
        moment_ref[:, columns] = moment
        high, low = split(moment)
        both = dot(left[...], high)
        value = both[:TILE_ROWS] + both[TILE_ROWS:] + dot(left[:TILE_ROWS], low)
        high, low = split(value)
        c_ref[:, j * NARROW : (j + 1) * NARROW] = (
            dot(high, right[0]) + dot(high, right[1]) + dot(low, right[0])
        )
    is_first = core == 0
    one, two = c_ref[:, :HALF], c_ref[:, HALF:]
    mine_ref[...] = jnp.where(is_first, one, two)
    theirs_ref[...] = jnp.where(is_first, two, one)
    for copy in others[2:]:
        copy.wait()


def band(momentum, gradient, weights, table, **order):
    part = ((TILE_ROWS, HALF), f32, VMEM)
    rows = ((HALF_ROWS, COLS), bf16, VMEM)
    return call(
        band_kernel,
        [(array, ANY) for array in (momentum, gradient, weights, table["left"], table["right"])],
        [((TILE_ROWS, BANDS), f32, VMEM), part, part, ((ROWS, COLS), f32, VMEM), rows, rows],
        scratch=[
            pltpu.VMEM((ROWS, COLS), bf16),
            pltpu.VMEM((2 * TILE_ROWS, ROWS), bf16),
            pltpu.VMEM((2, WIDE, NARROW), bf16),
            pltpu.SemaphoreType.DMA((2 * N_WIDE + 4,)),
        ],
        name="band",
        **order,
    )


def field_of(band, left_t, right_t):
    high, low = split(band)
    value = dot(jnp.concatenate([high, low, high], axis=1), right_t)
    high, low = split(value)
    return dot(left_t, jnp.concatenate([high, low, high], axis=0))


def momentum_kernel(moment_ref, c_ref, left_ref, right_ref, out_ref):
    columns = pl.ds(pl.multiple_of(pl.program_id(0) * WIDE, WIDE), WIDE)
    bands = pl.ds(pl.multiple_of(pl.program_id(0) * NARROW, NARROW), NARROW)
    out_ref[0] = moment_ref[:, columns] - field_of(
        c_ref[:, bands], left_ref[...], right_ref[...]
    )


def momentum_less_band(moment, coeffs, table, **order):
    return call(
        momentum_kernel,
        [
            (moment, VMEM),
            (coeffs, VMEM),
            (table["left_t"], VMEM),
            (table["right_t"], VMEM),
        ],
        [((1, ROWS, COLS), f32, column_block_of_one(ROWS, WIDE))],
        grid=(COLS // WIDE,),
        name="momentum_less_band",
        **order,
    )


def update_kernel(mine_ref, theirs_ref, left_ref, right_ref, out_ref, total):
    j = pl.program_id(0)

    @pl.when(j == 0)
    def _():
        is_first = core_of() == 0
        mine, theirs = mine_ref[...] / N_REP, theirs_ref[...] / N_REP
        first = jnp.where(is_first, mine, theirs)
        second = jnp.where(is_first, theirs, mine)
        full = jnp.concatenate([first, second], axis=1)
        for k in range(5):
            total[k] = full[:, k * NARROW : (k + 1) * NARROW]

    out_ref[...] = field_of(total[j], left_ref[...], right_ref[...])


def update_of(mine, theirs, table, **order):
    return call(
        update_kernel,
        [
            (mine, whole((TILE_ROWS, HALF))),
            (theirs, whole((TILE_ROWS, HALF))),
            (table["left_t"], whole((ROWS, 3 * TILE_ROWS))),
            (table["right_t"], whole((3 * NARROW, WIDE))),
        ],
        [((ROWS, COLS), f32, column_block(ROWS, WIDE))],
        scratch=[pltpu.VMEM((5, TILE_ROWS, NARROW), f32)],
        grid=(COLS // WIDE,),
        name="update",
        **order,
    )


SIDES = (3, 0, 1, 2)


def input_band_kernel(x_ref, pair_ref, high_ref, low_ref, turned_ref, held, pair, sems):
    def copy(j):
        columns = pl.ds(j * WIDE, WIDE)
        return pltpu.make_async_copy(x_ref.at[0, :, columns], held.at[:, columns], sems.at[j])

    table = pltpu.make_async_copy(pair_ref, pair, sems.at[N_WIDE])
    table.start()
    for j in range(N_WIDE):
        copy(j).start()
    table.wait()
    for j in range(N_WIDE):
        copy(j).wait()
        both = dot(held[:, j * WIDE : (j + 1) * WIDE], pair[...])
        bands = slice(j * NARROW, (j + 1) * NARROW)
        high_ref[:, bands], low_ref[:, bands] = split(both[:, :NARROW] + both[:, NARROW:])
    shard = lax.axis_index("fsdp")
    here, z = shard // 4, lax.rem(shard, 4)
    wide = COLS // 2
    for k in range(4):

        @pl.when(z == k)
        def _():
            for part, x in enumerate((here, 1 - here)):
                source = held[:, pl.ds(pl.multiple_of(x * wide, NARROW), wide)]
                starts = [(k + side) % 4 * ROWS for side in SIDES]
                turned_ref[:, part * wide : (part + 1) * wide] = jnp.concatenate(
                    [source[:, start : start + ROWS] for start in starts], axis=1
                )


def input_band(inputs, table, **order):
    part = ((TOKENS, BANDS), bf16, VMEM)
    return call(
        input_band_kernel,
        [(inputs, ANY), (table["right_pair"], ANY)],
        [part, part, ((TOKENS, COLS), bf16, VMEM)],
        scratch=[
            pltpu.VMEM((TOKENS, COLS), bf16),
            pltpu.VMEM((WIDE, 2 * NARROW), bf16),
            pltpu.SemaphoreType.DMA((N_WIDE + 1,)),
        ],
        name="input_band",
        **order,
    )


def sum_kernel(*refs):
    total = refs[0][...]
    for ref in refs[1:-1]:
        total += ref[...]
    refs[-1][...] = total


def sum_of(parts, name, **order):
    return call(
        sum_kernel,
        [(part, VMEM) for part in parts],
        [(parts[0].shape, f32, VMEM)],
        name=name,
        **order,
    )


def both_kernel(own_ref, other_ref, out_ref):
    is_first = lax.axis_index("fsdp") < 4
    own, other = own_ref[...], other_ref[...]
    out_ref[:TILE_ROWS] = jnp.where(is_first, own, other)
    out_ref[TILE_ROWS:] = jnp.where(is_first, other, own)


def both_of(own, other, **order):
    return call(
        both_kernel,
        [(own, VMEM), (other, VMEM)],
        [((2 * TILE_ROWS, HALF), f32, VMEM)],
        name="both",
        **order,
    )


def pair_kernel(one_ref, two_ref, own_ref, pair_ref):
    total = one_ref[...] + two_ref[...]
    is_first = lax.axis_index("fsdp") < 4
    own_ref[...] = jnp.where(is_first, total[:TILE_ROWS], total[TILE_ROWS:])
    pair_ref[...] = total.astype(bf16)


def pair_of(one, two, **order):
    return call(
        pair_kernel,
        [(one, VMEM), (two, VMEM)],
        [((TILE_ROWS, HALF), f32, VMEM), ((2 * TILE_ROWS, HALF), bf16, VMEM)],
        name="pair",
        **order,
    )


def quad_kernel(pair_ref, other_ref, out_ref):
    is_even = lax.rem(lax.axis_index("fsdp"), 2) == 0
    rows = 2 * TILE_ROWS
    pair, other = pair_ref[...], other_ref[...]
    out_ref[:rows] = jnp.where(is_even, pair, other)
    out_ref[rows:] = jnp.where(is_even, other, pair)


def quad_of(pair, other, **order):
    return call(
        quad_kernel,
        [(pair, VMEM), (other, VMEM)],
        [((4 * TILE_ROWS, HALF), bf16, VMEM)],
        name="quad",
        **order,
    )


def hand_on_kernel():
    pass


def hand_on(arrays, after, name):
    return call(hand_on_kernel, [], [], name=name, after=after, through=arrays)[1:]


def change_kernel(high_ref, low_ref, here_ref, there_ref, s_here_ref, s_there_ref, out_ref):
    is_first = core_of() == 0
    is_low = lax.rem(lax.axis_index("fsdp"), 4) < 2
    here = here_ref[...], s_here_ref[...]
    there = there_ref[...], s_there_ref[...]
    for half in range(2):
        near = jnp.where(is_first, here[half], here[1 - half])
        far = jnp.where(is_first, there[half], there[1 - half])
        one, two = jnp.where(is_low, near, far), jnp.where(is_low, far, near)
        blocks = [part[k * TILE_ROWS : (k + 1) * TILE_ROWS] for part in (one, two) for k in range(4)]
        total = jnp.concatenate([blocks[2 * z + x] for x in range(2) for z in range(4)], axis=0)
        value = dot(high_ref[...], total) + dot(low_ref[...], total)
        for k in range(5):
            high, low = split(value[:, k * 64 : (k + 1) * 64])
            start = (half * 5 + k) * 256
            out_ref[:, start : start + 256] = jnp.concatenate([high, low, high, low], axis=1)


def change_of(high, low, quads, **order):
    return call(
        change_kernel,
        [(array, VMEM) for array in (high, low, *quads)],
        [((TOKENS, COLS), bf16, VMEM)],
        name="change",
        **order,
    )


BLOCK = 512
N_BLOCKS = COLS // BLOCK


def beside(core, first, s_first, second, s_second, columns):
    is_first = core == 0
    a, sa, b, sb = (ref[:, columns] for ref in (first, s_first, second, s_second))
    before = [jnp.where(is_first, a, sa), jnp.where(is_first, b, sb)]
    behind = [jnp.where(is_first, sb, b), jnp.where(is_first, sa, a)]
    return before, behind


def in_order(core, one, other, columns):
    is_first = core == 0
    a, b = one[:, columns], other[:, columns]
    return [jnp.where(is_first, a, b), jnp.where(is_first, b, a)]


def own_kernel(x_ref, w_ref, z0, sz0, z1, sz1, z2, sz2, out_ref):
    core = core_of()
    for n in range(N_BLOCKS):
        columns = slice(n * BLOCK, (n + 1) * BLOCK)
        before, behind = beside(core, z0, sz0, z1, sz1, columns)
        rows = before + [w_ref[:, columns]] + behind + in_order(core, z2, sz2, columns)
        out_ref[:, columns] = dot(x_ref[:, : 4 * ROWS], jnp.concatenate(rows, axis=0))


def own_product(turned, pieces, **order):
    return call(
        own_kernel,
        [(array, VMEM) for array in (turned, *pieces)],
        [((TOKENS, COLS), f32, VMEM)],
        name="own_product",
        **order,
    )


def rest_kernel(
    x_ref, acc_ref, change_ref, step_ref,
    x0, sx0, z0, sz0, z1, sz1, top, s_top, low, s_low, out_ref,
):
    core = core_of()
    columns = pl.ds(pl.multiple_of(pl.program_id(0) * BLOCK, BLOCK), BLOCK)
    before, behind = beside(core, z0, sz0, z1, sz1, columns)
    tops, lows = in_order(core, top, s_top, columns), in_order(core, low, s_low, columns)
    rows = before + in_order(core, x0, sx0, columns) + behind
    rows += [tops[0], lows[0], tops[1], lows[1]]
    change = change_ref[:, columns]
    steps = [dot(change[:, k : k + 256], step_ref[...]) for k in (0, 256)]
    value = dot(x_ref[:, 4 * ROWS :], jnp.concatenate(rows, axis=0))
    out_ref[0] = (acc_ref[:, columns] + value + jnp.concatenate(steps, axis=1)).astype(bf16)


def rest_product(turned, acc, change, pieces, table, **order):
    return call(
        rest_kernel,
        [(array, VMEM) for array in (turned, acc, change, table["step"], *pieces)],
        [((1, TOKENS, COLS), bf16, column_block_of_one(TOKENS, BLOCK))],
        grid=(N_BLOCKS,),
        name="rest_product",
        **order,
    )


def swapped(value, axis, step):
    pairs = []
    for device in range(128):
        place = list(place_of(device))
        place[axis] = 3 - place[axis] if step else place[axis] ^ 1
        pairs.append((device, device_at(*place)))
    return lax.ppermute(value, BOTH, pairs)


def shards(momentum, gradient, weights, inputs):
    table = {
        name: pltpu.with_memory_space_constraint(jnp.asarray(value), pltpu.HBM)
        if name in ("left", "right", "right_pair")
        else value
        for name, value in tables().items()
    }
    momentum, gradient, weights, inputs = (
        pltpu.with_memory_space_constraint(array, pltpu.HBM)
        for array in (momentum, gradient, weights, inputs)
    )

    coeffs, mine, theirs, moment, first, second, _ = band(momentum, gradient, weights, table)
    z0 = along_z(first)
    x0 = along_x(first)
    z1 = along_z(second)
    chip, _ = sum_of([mine, across(theirs)], "chip_sum")
    half_y = swapped(chip, 1, 0)
    high, low, turned, done = input_band(inputs, table, after=[chip])
    half_sum, _, z0, x0 = sum_of(
        [chip, half_y], "half_y_sum", after=[done], through=[z0, x0]
    )
    rest_y = swapped(half_sum, 1, 1)
    xz0 = along_x(z0)
    z2 = along_z(z0)
    sz0 = across(z0)
    column, _, z1, sz0, x0 = sum_of([half_sum, rest_y], "y_sum", through=[z1, sz0, x0])
    half_x = swapped(column, 0, 0)
    xz1 = along_x(z1)
    sz1 = across(z1)
    both, _, xz0, z2, x0, sz1 = both_of(column, half_x, through=[xz0, z2, x0, sz1])
    rest_x = swapped(both, 0, 1)
    sx0, sz2, sxz0 = across(x0), across(z2), across(xz0)
    new_momentum, done = momentum_less_band(moment, coeffs, table, after=[both])
    own, pair, _, xz1, sx0, sz2, sxz0, z2, xz0 = pair_of(
        both, rest_x, after=[done], through=[xz1, sx0, sz2, sxz0, z2, xz0]
    )
    half_z = swapped(pair, 2, 0)
    s_own, sxz1 = across(own), across(xz1)
    xz2 = along_x(z2[:QUARTER])
    z3 = along_z(xz0[QUARTER:])
    update, done = update_of(own, s_own, table, after=[pair])
    quad, _, sxz1 = quad_of(pair, half_z, after=[done], through=[sxz1])
    rest_z = swapped(quad, 2, 1)
    s_quad = across(quad)
    acc, done, s_quad = own_product(
        turned, [weights, z0, sz0, z1, sz1, z2, sz2], after=[quad], through=[s_quad]
    )
    rest_z, xz2, z3 = hand_on([rest_z, xz2, z3], [done], "after_own_product")
    change, _ = change_of(high, low, [quad, rest_z, s_quad, across(rest_z)])
    result, _ = rest_product(
        turned,
        acc,
        change,
        [x0, sx0, xz0, sxz0, xz1, sxz1, xz2, across(xz2), z3, across(z3)],
        table,
    )
    return (new_momentum, update, result)


def solution(mesh):
    placed = (
        P("rep", "fsdp", None),
        P("rep", "fsdp", None),
        P("fsdp", None),
        P("rep", "fsdp", None),
    )
    return jax.shard_map(
        shards,
        mesh=mesh,
        in_specs=placed,
        out_specs=(P("rep", "fsdp", None), P("fsdp", None), P("rep", "fsdp", None)),
        check_vma=False,
    )
```

time: 358 us -> 88.8 us (0.25)
  waiting for transfers between devices: 252 us -> 19.1 us
  matrix products: 51.3 us -> 0 us
  Pallas kernels: 0 us -> 36.8 us
  starting transfers between devices: 0.22 us -> 31.9 us
  local copies, waits for them, and re-layouts: 31.3 us -> 0.07 us
  between operations: 14.1 us -> 0.74 us
  other arithmetic: 8.29 us -> 0 us
    psum x1 -> x0, waiting for transfers between devices: 127 us -> none  [shards(): mean_band = lax.psum(coeffs, 'rep') / lax.axis_size('rep')]
    all_gather x1 -> x0, waiting for transfers between devices: 124 us -> none  [shards(): lax.all_gather(new_weights, 'fsdp', axis=0, tiled=True)]
    dot_general x7 -> x0, matrix products: 51.3 us -> none  [the longest x2 24.1 us: right_inverse(): jnp.dot(partial_value, columns.T, precision=highest, preferred_element_ty...]
    pallas_call x0 -> x14, Pallas kernels: none -> 36.8 us  [call(): pl.pallas_call(body, grid=grid, out_shape=tuple((jax.ShapeDtypeStruct(sha...]
    ppermute x0 -> x26, starting transfers between devices: none -> 31.9 us  [the longest x20 20.7 us: moved(): return lax.ppermute(value, BOTH, pairs)]
    select_n x2 -> x0, local copies, waits for them, and re-layouts: 23.5 us -> none  [column_table(): return jnp.where(same_block, repeated, jnp.zeros_like(repeated))]
    ppermute x0 -> x26, waiting for transfers between devices: none -> 19.1 us  [the longest x20 11.4 us: moved(): return lax.ppermute(value, BOTH, pairs)]
    unnamed x9 -> x6, local copies, waits for them, and re-layouts: 7.82 us -> 0.01 us
  transfers between devices with their start and end apart: 2 -> 26, of which waited for: 2 -> 11; matrix products, arithmetic and copies ran while one was open for 7% -> 0% of each run, Pallas kernels for 0% -> 27%
where the time goes in v1:
time: 88.8 us; the launch traced here: 88.6 us
  Pallas kernels  36.8 us (41%)
  starting transfers between devices  31.9 us (36%)
  waiting for transfers between devices  19.1 us (22%)
    pallas_call x14, Pallas kernels, call(): pl.pallas_call(body, grid=grid, out_shape=tuple((jax.ShapeDtypeStruct(sha...  36.8 us
    ppermute x20, starting transfers between devices, moved(): return lax.ppermute(value, BOTH, pairs)  20.7 us
    ppermute x20, waiting for transfers between devices, moved(): return lax.ppermute(value, BOTH, pairs)  11.4 us
    ppermute x6, starting transfers between devices, swapped(): return lax.ppermute(value, BOTH, pairs)  11.2 us
    ppermute x6, waiting for transfers between devices, swapped(): return lax.ppermute(value, BOTH, pairs)  7.74 us
  transfers between devices with their start and end apart: 26, of which 11 were waited for; matrix products, arithmetic and copies ran while one was open for 0% of the time, Pallas kernels for 27%

profile of v1, /device:TPU:1, one launch (start us, length us, event | category | flops | bytes accessed | tf_op | source)
XLA Modules:
  0.0 88.6 jit_solution(515531869862387824)
XLA Ops:
  0.6 4.7 %band.1 = (f32[80,640]{1,0:T(8,128)S(1)}, f32[80,320]{1,0:T(8,128)S(1)}, f32[80,320]{1,0:T(8,128)S(1)}, f32[320,2560]{1,0:T(8,128)S(1)}, bf16[160,2560]{1,0:T(8,...) custom-call(f32[1,320,2560]{2,1,0:T(8,128)} %refs_0_.2, bf16[1,320,2560]{2,1,0:T(8,128)(2,1)} %refs_1_.3, ...), custom_call_target="tpu_custom_call" | custom-call | flops 1 | bytes 1 | tf_op jit(solution)/shard_map/band/pallas_call | solution.py:125
  5.3 4.7 %collective-permute-start.2 = (bf16[160,2560]{1,0:T(8,128)(2,1)S(1)}, bf16[160,2560]{1,0:T(8,128)(2,1)S(1)}, u32[]{:S(2)}, u32[]{:S(2)}) collective-permute-start(bf16[160,2560]{1,0:T(8,128)(2,1)S(1)} %get-tuple-element.54), channel_id=1, source_target_pairs={{0,1},{1,2},{2,3},{3,0},{4,5},{5,6},{6,7},{7,4},{8,11},{9,8},{10,9... | collective-permute-start | bytes 2457608 | tf_op jit(solution)/shard_map/ppermute | solution.py:42
  10.0 2.5 %collective-permute-start.3 = (bf16[160,2560]{1,0:T(8,128)(2,1)S(1)}, bf16[160,2560]{1,0:T(8,128)(2,1)S(1)}, u32[]{:S(2)}, u32[]{:S(2)}) collective-permute-start(bf16[160,2560]{1,0:T(8,128)(2,1)S(1)} %get-tuple-element.54), channel_id=1, source_target_pairs={{0,4},{1,5},{2,6},{3,7},{4,16},{5,17},{6,18},{7,19},{8,28},{9,29},... | collective-permute-start | bytes 2457608 | tf_op jit(solution)/shard_map/ppermute | solution.py:42
  12.5 0.0 collective-permute-start
  12.5 1.3 %collective-permute-done.refs_1_ = f32[80,320]{1,0:T(8,128)S(1)} collective-permute-done((f32[80,320]{1,0:T(8,128)S(1)}, f32[80,320]{1,0:T(8,128)S(1)}, u32[]{:S(2)}, u32[]{:S(2)}) %collective-permute-start) | collective-permute-done | bytes 102432 | tf_op jit(solution)/shard_map/ppermute | solution.py:42
  13.8 0.6 chip_sum.1
  14.4 1.3 %collective-permute-start.1 = (f32[80,320]{1,0:T(8,128)S(1)}, f32[80,320]{1,0:T(8,128)S(1)}, u32[]{:S(2)}, u32[]{:S(2)}) collective-permute-start(f32[80,320]{1,0:T(8,128)S(1)} %get-tuple-element.52.refs_2_.refs_0_), channel_id=1, source_target_pairs={{0,32},{1,33},{2,34},{3,35},{4,36},{5,37},{6,38},{7,39},{8,40},{9,... | collective-permute-start | bytes 307208 | tf_op jit(solution)/shard_map/ppermute | solution.py:510
  15.7 0.1 collective-permute-start.5
  15.8 4.5 %input_band.1 = (bf16[640,640]{1,0:T(8,128)(2,1)S(1)}, bf16[640,640]{1,0:T(8,128)(2,1)S(1)}, bf16[640,2560]{1,0:T(8,128)(2,1)S(1)}, f32[8,128]{1,0:T(8,128)S(1)}) custom-call(bf16[1,640,2560]{2,1,0:T(8,128)(2,1)} %refs_0_.3, bf16[512,256]{1,0:T(8,128)(2,1)} %constant.14.clone.refs_1_, f32[80,320]{1,0:T(8,128)S(1)} %get-tuple-element.52.refs_2_.refs_0_), custom_call_target="tpu_custom_call" | custom-call | flops 1 | bytes 1 | tf_op jit(solution)/shard_map/input_band/pallas_call | solution.py:125
  20.3 0.0 collective-permute-done.1.refs_1_
  20.3 0.0 collective-permute-done.2.refs_3_
  20.3 1.4 %collective-permute-done.3.refs_4_ = bf16[160,2560]{1,0:T(8,128)(2,1)S(1)} collective-permute-done((bf16[160,2560]{1,0:T(8,128)(2,1)S(1)}, bf16[160,2560]{1,0:T(8,128)(2,1)S(1)}, u32[]{:S(2)}, u32[]{:S(2)}) %collective-permute-start.3) | collective-permute-done | bytes 819232 | tf_op jit(solution)/shard_map/ppermute | solution.py:42
  21.7 0.6 half_y_sum.1
  22.4 0.6 collective-permute-start.6
  23.0 2.7 %collective-permute-start.4 = (f32[80,320]{1,0:T(8,128)S(1)}, f32[80,320]{1,0:T(8,128)S(1)}, u32[]{:S(2)}, u32[]{:S(2)}) collective-permute-start(f32[80,320]{1,0:T(8,128)S(1)} %get-tuple-element.55.refs_0_), channel_id=1, source_target_pairs={{0,96},{1,97},{2,98},{3,99},{4,100},{5,101},{6,102},{7,103},{8,104... | collective-permute-start | bytes 307208 | tf_op jit(solution)/shard_map/ppermute | solution.py:510
  25.7 2.8 %collective-permute-start.8 = (bf16[160,2560]{1,0:T(8,128)(2,1)S(1)}, bf16[160,2560]{1,0:T(8,128)(2,1)S(1)}, u32[]{:S(2)}, u32[]{:S(2)}) collective-permute-start(bf16[160,2560]{1,0:T(8,128)(2,1)S(1)} %get-tuple-element.57.refs_2_), channel_id=1, source_target_pairs={{0,4},{1,5},{2,6},{3,7},{4,16},{5,17},{6,18},{7,19},{8,28},{9,29},... | collective-permute-start | bytes 2457608 | tf_op jit(solution)/shard_map/ppermute | solution.py:42
  28.5 0.4 collective-permute-start.9
  28.9 0.0 collective-permute-done.5.refs_2_
  28.9 0.4 collective-permute-done.4.refs_1_
  29.3 0.0 collective-permute-done.6.refs_3_
  29.3 0.6 y_sum.1
  29.9 0.8 collective-permute-start.10
  30.7 1.2 %collective-permute-start.7 = (f32[80,320]{1,0:T(8,128)S(1)}, f32[80,320]{1,0:T(8,128)S(1)}, u32[]{:S(2)}, u32[]{:S(2)}) collective-permute-start(f32[80,320]{1,0:T(8,128)S(1)} %get-tuple-element.59.refs_0_), channel_id=1, source_target_pairs={{0,4},{1,5},{2,6},{3,7},{4,0},{5,1},{6,2},{7,3},{8,12},{9,13},{10,... | collective-permute-start | bytes 307208 | tf_op jit(solution)/shard_map/ppermute | solution.py:510
  31.9 1.8 %collective-permute-start.12 = (bf16[160,2560]{1,0:T(8,128)(2,1)S(1)}, bf16[160,2560]{1,0:T(8,128)(2,1)S(1)}, u32[]{:S(2)}, u32[]{:S(2)}) collective-permute-start(bf16[160,2560]{1,0:T(8,128)(2,1)S(1)} %get-tuple-element.61.refs_4_), channel_id=1, source_target_pairs={{0,4},{1,5},{2,6},{3,7},{4,16},{5,17},{6,18},{7,19},{8,28},{9,29},... | collective-permute-start | bytes 2457608 | tf_op jit(solution)/shard_map/ppermute | solution.py:42
  33.7 4.8 %collective-permute-done.8.refs_2_ = bf16[160,2560]{1,0:T(8,128)(2,1)S(1)} collective-permute-done((bf16[160,2560]{1,0:T(8,128)(2,1)S(1)}, bf16[160,2560]{1,0:T(8,128)(2,1)S(1)}, u32[]{:S(2)}, u32[]{:S(2)}) %collective-permute-start.8) | collective-permute-done | bytes 819232 | tf_op jit(solution)/shard_map/ppermute | solution.py:42
  38.5 1.5 %collective-permute-done.9.refs_3_ = bf16[160,2560]{1,0:T(8,128)(2,1)S(1)} collective-permute-done((bf16[160,2560]{1,0:T(8,128)(2,1)S(1)}, bf16[160,2560]{1,0:T(8,128)(2,1)S(1)}, u32[]{:S(2)}, u32[]{:S(2)}) %collective-permute-start.9) | collective-permute-done | bytes 819232 | tf_op jit(solution)/shard_map/ppermute | solution.py:42
  40.0 0.0 collective-permute-done.7.refs_1_
  40.0 0.0 collective-permute-done.10.refs_5_
  40.0 0.6 both.1
  40.6 0.7 collective-permute-start.13
  41.3 0.0 collective-permute-start.14
  41.3 0.5 collective-permute-start.15
  41.8 3.6 %collective-permute-start.11 = (f32[160,320]{1,0:T(8,128)S(1)}, f32[160,320]{1,0:T(8,128)S(1)}, u32[]{:S(2)}, u32[]{:S(2)}) collective-permute-start(f32[160,320]{1,0:T(8,128)S(1)} %get-tuple-element.62.refs_4_.refs_0_), channel_id=1, source_target_pairs={{0,20},{1,21},{2,22},{3,23},{4,16},{5,17},{6,18},{7,19},{8,28},{9,... | collective-permute-start | bytes 614408 | tf_op jit(solution)/shard_map/ppermute | solution.py:510
  45.4 3.8 %momentum_less_band.1 = (f32[1,320,2560]{2,1,0:T(8,128)}, f32[8,128]{1,0:T(8,128)S(1)}) custom-call(f32[320,2560]{1,0:T(8,128)S(1)} %get-tuple-element.48.refs_0_, f32[80,640]{1,0:T(8,128)S(1)} %get-tuple-element.49.refs_1_, bf16[320,240]{1,0:T(8,128)(2,1)S(1)} %copy-done.1, bf16[384,512]{1,0:T(8,128)(2,1)S(1)} %copy-done, ...), custom_call_target="tpu_custom_call" | custom-call | flops 1 | bytes 1 | tf_op jit(solution)/shard_map/momentum_less_band/pallas_call | solution.py:125
  49.2 0.0 collective-permute-done.12.refs_3_
  49.2 2.7 %collective-permute-done.11.refs_1_ = f32[160,320]{1,0:T(8,128)S(1)} collective-permute-done((f32[160,320]{1,0:T(8,128)S(1)}, f32[160,320]{1,0:T(8,128)S(1)}, u32[]{:S(2)}, u32[]{:S(2)}) %collective-permute-start.11) | collective-permute-done | bytes 204832 | tf_op jit(solution)/shard_map/ppermute | solution.py:510
  52.0 0.0 collective-permute-done.13.refs_4_
  52.0 0.0 collective-permute-done.14.refs_5_
  52.0 0.0 collective-permute-done.15.refs_6_
  52.0 0.6 pair.1
  52.6 2.0 %collective-permute-start.18 = (bf16[160,2560]{1,0:T(8,128)(2,1)S(1)}, bf16[160,2560]{1,0:T(8,128)(2,1)S(1)}, u32[]{:S(2)}, u32[]{:S(2)}) collective-permute-start(bf16[160,2560]{1,0:T(8,128)(2,1)S(1)} %get-tuple-element.77.refs_8_), channel_id=1, source_target_pairs={{0,8},{1,9},{2,10},{3,11},{4,12},{5,13},{6,14},{7,15},{8,0},{9,1},... | collective-permute-start | bytes 2457608 | tf_op jit(solution)/shard_map/ppermute | solution.py:42
  54.6 1.6 %collective-permute-start.21 = (bf16[80,2560]{1,0:T(8,128)(2,1)S(1)}, bf16[80,2560]{1,0:T(8,128)(2,1)S(1)}, u32[]{:S(2)}, u32[]{:S(2)}) collective-permute-start(bf16[80,2560]{1,0:T(8,128)(2,1)S(1)} %slice.6), channel_id=1, source_target_pairs={{0,4},{1,5},{2,6},{3,7},{4,16},{5,17},{6,18},{7,19},{8,28},{9,29},... | collective-permute-start | bytes 1228808 | tf_op jit(solution)/shard_map/ppermute | solution.py:42
  56.3 0.1 collective-permute-start.22
  56.4 0.2 collective-permute-start.16
  56.6 1.2 %collective-permute-start.17 = (bf16[160,320]{1,0:T(8,128)(2,1)S(1)}, bf16[160,320]{1,0:T(8,128)(2,1)S(1)}, u32[]{:S(2)}, u32[]{:S(2)}) collective-permute-start(bf16[160,320]{1,0:T(8,128)(2,1)S(1)} %get-tuple-element.69.refs_4_.refs_0_), channel_id=1, source_target_pairs={{0,1},{1,0},{2,3},{3,2},{4,5},{5,4},{6,7},{7,6},{8,9},{9,8},{10,11... | collective-permute-start | bytes 307208 | tf_op jit(solution)/shard_map/ppermute | solution.py:510
  57.8 0.1 collective-permute-done.16.refs_1_
  58.0 3.9 %update.1 = (f32[320,2560]{1,0:T(8,128)}, f32[8,128]{1,0:T(8,128)S(1)}) custom-call(f32[80,320]{1,0:T(8,128)S(1)} %get-tuple-element.68.refs_0_, f32[80,320]{1,0:T(8,128)S(1)} %collective-permute-done.16.refs_1_, bf16[320,240]{1,0:T(8,128)(2,1)S(1)} %copy-done.1, bf16[384,512]{1,0:T(8,128)(2,1)S(1)} %copy-done, ...), custom_call_target="tpu_custom_call" | custom-call | flops 1 | bytes 1 | tf_op jit(solution)/shard_map/update/pallas_call | solution.py:125
  61.9 3.9 %collective-permute-done.17.refs_1_ = bf16[160,320]{1,0:T(8,128)(2,1)S(1)} collective-permute-done((bf16[160,320]{1,0:T(8,128)(2,1)S(1)}, bf16[160,320]{1,0:T(8,128)(2,1)S(1)}, u32[]{:S(2)}, u32[]{:S(2)}) %collective-permute-start.17) | collective-permute-done | bytes 102432 | tf_op jit(solution)/shard_map/ppermute | solution.py:510
  65.8 0.0 collective-permute-done.18.refs_3_
  65.8 0.6 quad.1
  66.4 1.2 %collective-permute-start.20 = (bf16[320,320]{1,0:T(8,128)(2,1)S(1)}, bf16[320,320]{1,0:T(8,128)(2,1)S(1)}, u32[]{:S(2)}, u32[]{:S(2)}) collective-permute-start(bf16[320,320]{1,0:T(8,128)(2,1)S(1)} %get-tuple-element.78.refs_8_.refs_2_), channel_id=1, source_target_pairs={{0,3},{1,2},{2,1},{3,0},{4,7},{5,6},{6,5},{7,4},{8,11},{9,10},{10,... | collective-permute-start | bytes 614408 | tf_op jit(solution)/shard_map/ppermute | solution.py:510
  67.6 0.3 collective-permute-done.19.refs_9_
  67.9 5.9 %own_product.1 = (f32[640,2560]{1,0:T(8,128)S(1)}, f32[8,128]{1,0:T(8,128)S(1)}, bf16[320,320]{1,0:T(8,128)(2,1)S(1)}) custom-call(bf16[640,2560]{1,0:T(8,128)(2,1)S(1)} %get-tuple-element.71.refs_0_, bf16[320,2560]{1,0:T(8,128)(2,1)} %refs_1_.4, bf16[160,2560]{1,0:T(8,128)(2,1)S(1)} %get-tuple-element.57.refs_2_, ...), custom_call_target="tpu_custom_call", output_to_operand_aliasing={{2}: (9, {})} | custom-call | flops 1 | bytes 1 | tf_op jit(solution)/shard_map/own_product/pallas_call | solution.py:125
  73.9 0.0 copy-start.2
  73.9 0.0 collective-permute-done.21.refs_2_
  73.9 0.7 collective-permute-done.20.refs_1_
  74.6 0.6 after_own_product.1
  75.2 1.4 %collective-permute-start.24 = (bf16[80,2560]{1,0:T(8,128)(2,1)S(1)}, bf16[80,2560]{1,0:T(8,128)(2,1)S(1)}, u32[]{:S(2)}, u32[]{:S(2)}) collective-permute-start(bf16[80,2560]{1,0:T(8,128)(2,1)S(1)} %get-tuple-element.90.refs_10_), channel_id=1, source_target_pairs={{0,8},{1,9},{2,10},{3,11},{4,12},{5,13},{6,14},{7,15},{8,0},{9,1},... | collective-permute-start | bytes 1228808 | tf_op jit(solution)/shard_map/ppermute | solution.py:42
  76.6 0.5 collective-permute-start.23
  77.1 1.8 %collective-permute-done.23.refs_5_ = bf16[320,320]{1,0:T(8,128)(2,1)S(1)} collective-permute-done((bf16[320,320]{1,0:T(8,128)(2,1)S(1)}, bf16[320,320]{1,0:T(8,128)(2,1)S(1)}, u32[]{:S(2)}, u32[]{:S(2)}) %collective-permute-start.23) | collective-permute-done | bytes 204832 | tf_op jit(solution)/shard_map/ppermute | solution.py:42
  78.9 2.8 %change.1 = (bf16[640,2560]{1,0:T(8,128)(2,1)S(1)}, f32[8,128]{1,0:T(8,128)}) custom-call(bf16[640,640]{1,0:T(8,128)(2,1)S(1)} %get-tuple-element.80.refs_0_, bf16[640,640]{1,0:T(8,128)(2,1)S(1)} %get-tuple-element.81.refs_1_, bf16[320,320]{1,0:T(8,128)(2,1)S(1)} %get-tuple-element.78.refs_8_.refs_2_, bf16[320,320]{1,0:T(8,128)(2,1)S(1)} %get-tuple-element.84.refs_3_, ...), custom_call_target="tpu_custom_call" | custom-call | flops 1 | bytes 1 | tf_op jit(solution)/shard_map/change/pallas_call | solution.py:125
  81.7 0.0 collective-permute-done.24.refs_11_
  81.7 0.0 collective-permute-done.25.refs_13_
  81.7 6.9 %rest_product.1 = (bf16[1,640,2560]{2,1,0:T(8,128)(2,1)}, f32[8,128]{1,0:T(8,128)}) custom-call(bf16[640,2560]{1,0:T(8,128)(2,1)S(1)} %get-tuple-element.71.refs_0_, f32[640,2560]{1,0:T(8,128)S(1)} %get-tuple-element.79.refs_1_, bf16[640,2560]{1,0:T(8,128)(2,1)S(1)} %get-tuple-element.86.refs_2_, bf16[256,256]{1,0:T(8,128)(2,1)S(1)} %copy-done.2, ...), custom_call_target="tpu_custom_call" | custom-call | flops 1 | bytes 1 | tf_op jit(solution)/shard_map/rest_product/pallas_call | solution.py:125
  (10 shorter events, 0.1 us)
Async XLA Ops:
  5.3 15.0 %collective-permute-start.2 = (bf16[160,2560]{1,0:T(8,128)(2,1)S(1)}, bf16[160,2560]{1,0:T(8,128)(2,1)S(1)}, u32[]{:S(2)}, u32[]{:S(2)}) collective-permute-start(bf16[160,2560]{1,0:T(8,128)(2,1)S(1)} %get-tuple-element.54), channel_id=1, source_target_pairs={{0,1},{1,2},{2,3},{3,0},{4,5},{5,6},{6,7},{7,4},{8,11},{9,8},{10,9... | collective-permute-start | bytes 2457608 | tf_op jit(solution)/shard_map/ppermute | solution.py:42
  10.0 11.8 %collective-permute-start.3 = (bf16[160,2560]{1,0:T(8,128)(2,1)S(1)}, bf16[160,2560]{1,0:T(8,128)(2,1)S(1)}, u32[]{:S(2)}, u32[]{:S(2)}) collective-permute-start(bf16[160,2560]{1,0:T(8,128)(2,1)S(1)} %get-tuple-element.54), channel_id=1, source_target_pairs={{0,4},{1,5},{2,6},{3,7},{4,16},{5,17},{6,18},{7,19},{8,28},{9,29},... | collective-permute-start | bytes 2457608 | tf_op jit(solution)/shard_map/ppermute | solution.py:42
  12.5 1.3 %collective-permute-start = (f32[80,320]{1,0:T(8,128)S(1)}, f32[80,320]{1,0:T(8,128)S(1)}, u32[]{:S(2)}, u32[]{:S(2)}) collective-permute-start(f32[80,320]{1,0:T(8,128)S(1)} %get-tuple-element.51), channel_id=1, source_target_pairs={{0,8},{1,9},{2,10},{3,11},{4,12},{5,13},{6,14},{7,15},{8,0},{9,1},... | collective-permute-start | bytes 307208 | tf_op jit(solution)/shard_map/ppermute | solution.py:42
  14.4 5.9 %collective-permute-start.1 = (f32[80,320]{1,0:T(8,128)S(1)}, f32[80,320]{1,0:T(8,128)S(1)}, u32[]{:S(2)}, u32[]{:S(2)}) collective-permute-start(f32[80,320]{1,0:T(8,128)S(1)} %get-tuple-element.52.refs_2_.refs_0_), channel_id=1, source_target_pairs={{0,32},{1,33},{2,34},{3,35},{4,36},{5,37},{6,38},{7,39},{8,40},{9,... | collective-permute-start | bytes 307208 | tf_op jit(solution)/shard_map/ppermute | solution.py:510
  15.7 13.2 %collective-permute-start.5 = (bf16[160,2560]{1,0:T(8,128)(2,1)S(1)}, bf16[160,2560]{1,0:T(8,128)(2,1)S(1)}, u32[]{:S(2)}, u32[]{:S(2)}) collective-permute-start(bf16[160,2560]{1,0:T(8,128)(2,1)S(1)} %get-tuple-element.56), channel_id=1, source_target_pairs={{0,1},{1,2},{2,3},{3,0},{4,5},{5,6},{6,7},{7,4},{8,11},{9,8},{10,9... | collective-permute-start | bytes 2457608 | tf_op jit(solution)/shard_map/ppermute | solution.py:42
  22.4 23.0 %copy-start = (bf16[384,512]{1,0:T(8,128)(2,1)S(1)}, bf16[384,512]{1,0:T(8,128)(2,1)}, u32[]{:S(2)}) copy-start(bf16[384,512]{1,0:T(8,128)(2,1)} %constant.16.clone.refs_3_) | copy-start | bytes 1179652
  22.4 23.0 %copy-start.1 = (bf16[320,240]{1,0:T(8,128)(2,1)S(1)}, bf16[320,240]{1,0:T(8,128)(2,1)}, u32[]{:S(2)}) copy-start(bf16[320,240]{1,0:T(8,128)(2,1)} %constant.15.clone.refs_2_) | copy-start | bytes 460804
  22.4 6.9 %collective-permute-start.6 = (bf16[160,2560]{1,0:T(8,128)(2,1)S(1)}, bf16[160,2560]{1,0:T(8,128)(2,1)S(1)}, u32[]{:S(2)}, u32[]{:S(2)}) collective-permute-start(bf16[160,2560]{1,0:T(8,128)(2,1)S(1)} %get-tuple-element.57.refs_2_), channel_id=1, source_target_pairs={{0,8},{1,9},{2,10},{3,11},{4,12},{5,13},{6,14},{7,15},{8,0},{9,1},... | collective-permute-start | bytes 2457608 | tf_op jit(solution)/shard_map/ppermute | solution.py:42
  23.0 6.3 %collective-permute-start.4 = (f32[80,320]{1,0:T(8,128)S(1)}, f32[80,320]{1,0:T(8,128)S(1)}, u32[]{:S(2)}, u32[]{:S(2)}) collective-permute-start(f32[80,320]{1,0:T(8,128)S(1)} %get-tuple-element.55.refs_0_), channel_id=1, source_target_pairs={{0,96},{1,97},{2,98},{3,99},{4,100},{5,101},{6,102},{7,103},{8,104... | collective-permute-start | bytes 307208 | tf_op jit(solution)/shard_map/ppermute | solution.py:510
  25.7 12.8 %collective-permute-start.8 = (bf16[160,2560]{1,0:T(8,128)(2,1)S(1)}, bf16[160,2560]{1,0:T(8,128)(2,1)S(1)}, u32[]{:S(2)}, u32[]{:S(2)}) collective-permute-start(bf16[160,2560]{1,0:T(8,128)(2,1)S(1)} %get-tuple-element.57.refs_2_), channel_id=1, source_target_pairs={{0,4},{1,5},{2,6},{3,7},{4,16},{5,17},{6,18},{7,19},{8,28},{9,29},... | collective-permute-start | bytes 2457608 | tf_op jit(solution)/shard_map/ppermute | solution.py:42
  28.5 11.5 %collective-permute-start.9 = (bf16[160,2560]{1,0:T(8,128)(2,1)S(1)}, bf16[160,2560]{1,0:T(8,128)(2,1)S(1)}, u32[]{:S(2)}, u32[]{:S(2)}) collective-permute-start(bf16[160,2560]{1,0:T(8,128)(2,1)S(1)} %get-tuple-element.57.refs_2_), channel_id=1, source_target_pairs={{0,1},{1,2},{2,3},{3,0},{4,5},{5,6},{6,7},{7,4},{8,11},{9,8},{10,9... | collective-permute-start | bytes 2457608 | tf_op jit(solution)/shard_map/ppermute | solution.py:42
  29.9 10.1 %collective-permute-start.10 = (bf16[160,2560]{1,0:T(8,128)(2,1)S(1)}, bf16[160,2560]{1,0:T(8,128)(2,1)S(1)}, u32[]{:S(2)}, u32[]{:S(2)}) collective-permute-start(bf16[160,2560]{1,0:T(8,128)(2,1)S(1)} %get-tuple-element.61.refs_4_), channel_id=1, source_target_pairs={{0,8},{1,9},{2,10},{3,11},{4,12},{5,13},{6,14},{7,15},{8,0},{9,1},... | collective-permute-start | bytes 2457608 | tf_op jit(solution)/shard_map/ppermute | solution.py:42
  30.7 9.3 %collective-permute-start.7 = (f32[80,320]{1,0:T(8,128)S(1)}, f32[80,320]{1,0:T(8,128)S(1)}, u32[]{:S(2)}, u32[]{:S(2)}) collective-permute-start(f32[80,320]{1,0:T(8,128)S(1)} %get-tuple-element.59.refs_0_), channel_id=1, source_target_pairs={{0,4},{1,5},{2,6},{3,7},{4,0},{5,1},{6,2},{7,3},{8,12},{9,13},{10,... | collective-permute-start | bytes 307208 | tf_op jit(solution)/shard_map/ppermute | solution.py:510
  31.9 17.4 %collective-permute-start.12 = (bf16[160,2560]{1,0:T(8,128)(2,1)S(1)}, bf16[160,2560]{1,0:T(8,128)(2,1)S(1)}, u32[]{:S(2)}, u32[]{:S(2)}) collective-permute-start(bf16[160,2560]{1,0:T(8,128)(2,1)S(1)} %get-tuple-element.61.refs_4_), channel_id=1, source_target_pairs={{0,4},{1,5},{2,6},{3,7},{4,16},{5,17},{6,18},{7,19},{8,28},{9,29},... | collective-permute-start | bytes 2457608 | tf_op jit(solution)/shard_map/ppermute | solution.py:42
  40.6 11.4 %collective-permute-start.13 = (bf16[160,2560]{1,0:T(8,128)(2,1)S(1)}, bf16[160,2560]{1,0:T(8,128)(2,1)S(1)}, u32[]{:S(2)}, u32[]{:S(2)}) collective-permute-start(bf16[160,2560]{1,0:T(8,128)(2,1)S(1)} %get-tuple-element.65.refs_4_), channel_id=1, source_target_pairs={{0,8},{1,9},{2,10},{3,11},{4,12},{5,13},{6,14},{7,15},{8,0},{9,1},... | collective-permute-start | bytes 2457608 | tf_op jit(solution)/shard_map/ppermute | solution.py:42
  41.3 10.7 %collective-permute-start.14 = (bf16[160,2560]{1,0:T(8,128)(2,1)S(1)}, bf16[160,2560]{1,0:T(8,128)(2,1)S(1)}, u32[]{:S(2)}, u32[]{:S(2)}) collective-permute-start(bf16[160,2560]{1,0:T(8,128)(2,1)S(1)} %get-tuple-element.66.refs_7_), channel_id=1, source_target_pairs={{0,8},{1,9},{2,10},{3,11},{4,12},{5,13},{6,14},{7,15},{8,0},{9,1},... | collective-permute-start | bytes 2457608 | tf_op jit(solution)/shard_map/ppermute | solution.py:42
  41.3 10.7 %collective-permute-start.15 = (bf16[160,2560]{1,0:T(8,128)(2,1)S(1)}, bf16[160,2560]{1,0:T(8,128)(2,1)S(1)}, u32[]{:S(2)}, u32[]{:S(2)}) collective-permute-start(bf16[160,2560]{1,0:T(8,128)(2,1)S(1)} %get-tuple-element.67.refs_8_), channel_id=1, source_target_pairs={{0,8},{1,9},{2,10},{3,11},{4,12},{5,13},{6,14},{7,15},{8,0},{9,1},... | collective-permute-start | bytes 2457608 | tf_op jit(solution)/shard_map/ppermute | solution.py:42
  41.8 10.2 %collective-permute-start.11 = (f32[160,320]{1,0:T(8,128)S(1)}, f32[160,320]{1,0:T(8,128)S(1)}, u32[]{:S(2)}, u32[]{:S(2)}) collective-permute-start(f32[160,320]{1,0:T(8,128)S(1)} %get-tuple-element.62.refs_4_.refs_0_), channel_id=1, source_target_pairs={{0,20},{1,21},{2,22},{3,23},{4,16},{5,17},{6,18},{7,19},{8,28},{9,... | collective-permute-start | bytes 614408 | tf_op jit(solution)/shard_map/ppermute | solution.py:510
  52.6 13.2 %collective-permute-start.18 = (bf16[160,2560]{1,0:T(8,128)(2,1)S(1)}, bf16[160,2560]{1,0:T(8,128)(2,1)S(1)}, u32[]{:S(2)}, u32[]{:S(2)}) collective-permute-start(bf16[160,2560]{1,0:T(8,128)(2,1)S(1)} %get-tuple-element.77.refs_8_), channel_id=1, source_target_pairs={{0,8},{1,9},{2,10},{3,11},{4,12},{5,13},{6,14},{7,15},{8,0},{9,1},... | collective-permute-start | bytes 2457608 | tf_op jit(solution)/shard_map/ppermute | solution.py:42
  54.6 19.2 %collective-permute-start.21 = (bf16[80,2560]{1,0:T(8,128)(2,1)S(1)}, bf16[80,2560]{1,0:T(8,128)(2,1)S(1)}, u32[]{:S(2)}, u32[]{:S(2)}) collective-permute-start(bf16[80,2560]{1,0:T(8,128)(2,1)S(1)} %slice.6), channel_id=1, source_target_pairs={{0,4},{1,5},{2,6},{3,7},{4,16},{5,17},{6,18},{7,19},{8,28},{9,29},... | collective-permute-start | bytes 1228808 | tf_op jit(solution)/shard_map/ppermute | solution.py:42
  56.3 17.6 %collective-permute-start.22 = (bf16[80,2560]{1,0:T(8,128)(2,1)S(1)}, bf16[80,2560]{1,0:T(8,128)(2,1)S(1)}, u32[]{:S(2)}, u32[]{:S(2)}) collective-permute-start(bf16[80,2560]{1,0:T(8,128)(2,1)S(1)} %slice.7), channel_id=1, source_target_pairs={{0,1},{1,2},{2,3},{3,0},{4,5},{5,6},{6,7},{7,4},{8,11},{9,8},{10,9... | collective-permute-start | bytes 1228808 | tf_op jit(solution)/shard_map/ppermute | solution.py:42
  56.4 1.6 %collective-permute-start.16 = (f32[80,320]{1,0:T(8,128)S(1)}, f32[80,320]{1,0:T(8,128)S(1)}, u32[]{:S(2)}, u32[]{:S(2)}) collective-permute-start(f32[80,320]{1,0:T(8,128)S(1)} %get-tuple-element.68.refs_0_), channel_id=1, source_target_pairs={{0,8},{1,9},{2,10},{3,11},{4,12},{5,13},{6,14},{7,15},{8,0},{9,1},... | collective-permute-start | bytes 307208 | tf_op jit(solution)/shard_map/ppermute | solution.py:42
  56.6 9.1 %collective-permute-start.17 = (bf16[160,320]{1,0:T(8,128)(2,1)S(1)}, bf16[160,320]{1,0:T(8,128)(2,1)S(1)}, u32[]{:S(2)}, u32[]{:S(2)}) collective-permute-start(bf16[160,320]{1,0:T(8,128)(2,1)S(1)} %get-tuple-element.69.refs_4_.refs_0_), channel_id=1, source_target_pairs={{0,1},{1,0},{2,3},{3,2},{4,5},{5,4},{6,7},{7,6},{8,9},{9,8},{10,11... | collective-permute-start | bytes 307208 | tf_op jit(solution)/shard_map/ppermute | solution.py:510
  66.4 1.5 %collective-permute-start.19 = (bf16[320,320]{1,0:T(8,128)(2,1)S(1)}, bf16[320,320]{1,0:T(8,128)(2,1)S(1)}, u32[]{:S(2)}, u32[]{:S(2)}) collective-permute-start(bf16[320,320]{1,0:T(8,128)(2,1)S(1)} %get-tuple-element.78.refs_8_.refs_2_), channel_id=1, source_target_pairs={{0,8},{1,9},{2,10},{3,11},{4,12},{5,13},{6,14},{7,15},{8,0},{9,1},... | collective-permute-start | bytes 614408 | tf_op jit(solution)/shard_map/ppermute | solution.py:42
  66.4 8.2 %collective-permute-start.20 = (bf16[320,320]{1,0:T(8,128)(2,1)S(1)}, bf16[320,320]{1,0:T(8,128)(2,1)S(1)}, u32[]{:S(2)}, u32[]{:S(2)}) collective-permute-start(bf16[320,320]{1,0:T(8,128)(2,1)S(1)} %get-tuple-element.78.refs_8_.refs_2_), channel_id=1, source_target_pairs={{0,3},{1,2},{2,1},{3,0},{4,7},{5,6},{6,5},{7,4},{8,11},{9,10},{10,... | collective-permute-start | bytes 614408 | tf_op jit(solution)/shard_map/ppermute | solution.py:510
  73.9 7.8 %copy-start.2 = (bf16[256,256]{1,0:T(8,128)(2,1)S(1)}, bf16[256,256]{1,0:T(8,128)(2,1)}, u32[]{:S(2)}) copy-start(bf16[256,256]{1,0:T(8,128)(2,1)} %constant.17.clone.refs_3_) | copy-start | bytes 393220
  75.2 6.5 %collective-permute-start.24 = (bf16[80,2560]{1,0:T(8,128)(2,1)S(1)}, bf16[80,2560]{1,0:T(8,128)(2,1)S(1)}, u32[]{:S(2)}, u32[]{:S(2)}) collective-permute-start(bf16[80,2560]{1,0:T(8,128)(2,1)S(1)} %get-tuple-element.90.refs_10_), channel_id=1, source_target_pairs={{0,8},{1,9},{2,10},{3,11},{4,12},{5,13},{6,14},{7,15},{8,0},{9,1},... | collective-permute-start | bytes 1228808 | tf_op jit(solution)/shard_map/ppermute | solution.py:42
  76.6 5.1 %collective-permute-start.25 = (bf16[80,2560]{1,0:T(8,128)(2,1)S(1)}, bf16[80,2560]{1,0:T(8,128)(2,1)S(1)}, u32[]{:S(2)}, u32[]{:S(2)}) collective-permute-start(bf16[80,2560]{1,0:T(8,128)(2,1)S(1)} %get-tuple-element.91.refs_12_), channel_id=1, source_target_pairs={{0,8},{1,9},{2,10},{3,11},{4,12},{5,13},{6,14},{7,15},{8,0},{9,1},... | collective-permute-start | bytes 1228808 | tf_op jit(solution)/shard_map/ppermute | solution.py:42
  76.6 2.3 %collective-permute-start.23 = (bf16[320,320]{1,0:T(8,128)(2,1)S(1)}, bf16[320,320]{1,0:T(8,128)(2,1)S(1)}, u32[]{:S(2)}, u32[]{:S(2)}) collective-permute-start(bf16[320,320]{1,0:T(8,128)(2,1)S(1)} %get-tuple-element.84.refs_3_), channel_id=1, source_target_pairs={{0,8},{1,9},{2,10},{3,11},{4,12},{5,13},{6,14},{7,15},{8,0},{9,1},... | collective-permute-start | bytes 614408 | tf_op jit(solution)/shard_map/ppermute | solution.py:42

commit v2 on v1

--- a/solution.py
+++ b/solution.py
@@ -112,7 +112,7 @@
     return pltpu.CompilerParams(vmem_limit_bytes=megabytes * 2**20)
 
 
-def call(kernel, ins, outs, scratch=(), grid=(), megabytes=24, name=None, after=(), through=()):
+def call(kernel, ins, outs, scratch=(), grid=(), megabytes=24, name=None, after=(), through=(), cost=1, held=()):
     n_in, n_out, n_extra = len(ins), len(outs), len(after) + len(through)
     token = ((8, 128), f32, whole((8, 128)) if grid else VMEM)
 
@@ -125,7 +125,10 @@
     return pl.pallas_call(
         body,
         grid=grid,
-        out_shape=tuple(jax.ShapeDtypeStruct(shape, dtype) for shape, dtype, _ in (*outs, token))
+        out_shape=tuple(
+            pltpu.VMEM(shape, dtype) if spec is VMEM and shape in held else jax.ShapeDtypeStruct(shape, dtype)
+            for shape, dtype, spec in (*outs, token)
+        )
         + tuple(jax.ShapeDtypeStruct(array.shape, array.dtype) for array in through),
         in_specs=[spec for _, spec in ins] + [ANY] * n_extra,
         out_specs=tuple(spec for _, _, spec in (*outs, token)) + (ANY,) * len(through),
@@ -134,7 +137,7 @@
             n_in + len(after) + k: n_out + 1 + k for k in range(len(through))
         },
         compiler_params=params(megabytes),
-        cost_estimate=pl.CostEstimate(flops=1, transcendentals=0, bytes_accessed=1),
+        cost_estimate=pl.CostEstimate(flops=cost, transcendentals=0, bytes_accessed=1),
         name=name,
     )(*[array for array, _ in ins], *after, *through)
 
@@ -227,11 +230,11 @@
 
 
 def momentum_kernel(moment_ref, c_ref, left_ref, right_ref, out_ref):
-    columns = pl.ds(pl.multiple_of(pl.program_id(0) * WIDE, WIDE), WIDE)
-    bands = pl.ds(pl.multiple_of(pl.program_id(0) * NARROW, NARROW), NARROW)
-    out_ref[0] = moment_ref[:, columns] - field_of(
-        c_ref[:, bands], left_ref[...], right_ref[...]
-    )
+    for j in range(N_WIDE):
+        columns, bands = slice(j * WIDE, (j + 1) * WIDE), slice(j * NARROW, (j + 1) * NARROW)
+        out_ref[0, :, columns] = moment_ref[:, columns] - field_of(
+            c_ref[:, bands], left_ref[...], right_ref[...]
+        )
 
 
 def momentum_less_band(moment, coeffs, table, **order):
@@ -243,42 +246,31 @@
             (table["left_t"], VMEM),
             (table["right_t"], VMEM),
         ],
-        [((1, ROWS, COLS), f32, column_block_of_one(ROWS, WIDE))],
-        grid=(COLS // WIDE,),
+        [((1, ROWS, COLS), f32, VMEM)],
         name="momentum_less_band",
-        **order,
-    )
-
-
-def update_kernel(mine_ref, theirs_ref, left_ref, right_ref, out_ref, total):
-    j = pl.program_id(0)
-
-    @pl.when(j == 0)
-    def _():
-        is_first = core_of() == 0
-        mine, theirs = mine_ref[...] / N_REP, theirs_ref[...] / N_REP
-        first = jnp.where(is_first, mine, theirs)
-        second = jnp.where(is_first, theirs, mine)
-        full = jnp.concatenate([first, second], axis=1)
-        for k in range(5):
-            total[k] = full[:, k * NARROW : (k + 1) * NARROW]
-
-    out_ref[...] = field_of(total[j], left_ref[...], right_ref[...])
+        held=[(1, ROWS, COLS)],
+        **order,
+    )
+
+
+def update_kernel(mine_ref, theirs_ref, left_ref, right_ref, out_ref):
+    is_first = core_of() == 0
+    mine, theirs = mine_ref[...] / N_REP, theirs_ref[...] / N_REP
+    first = jnp.where(is_first, mine, theirs)
+    second = jnp.where(is_first, theirs, mine)
+    full = jnp.concatenate([first, second], axis=1)
+    for j in range(N_WIDE):
+        columns, bands = slice(j * WIDE, (j + 1) * WIDE), slice(j * NARROW, (j + 1) * NARROW)
+        out_ref[:, columns] = field_of(full[:, bands], left_ref[...], right_ref[...])
 
 
 def update_of(mine, theirs, table, **order):
     return call(
         update_kernel,
-        [
-            (mine, whole((TILE_ROWS, HALF))),
-            (theirs, whole((TILE_ROWS, HALF))),
-            (table["left_t"], whole((ROWS, 3 * TILE_ROWS))),
-            (table["right_t"], whole((3 * NARROW, WIDE))),
-        ],
-        [((ROWS, COLS), f32, column_block(ROWS, WIDE))],
-        scratch=[pltpu.VMEM((5, TILE_ROWS, NARROW), f32)],
-        grid=(COLS // WIDE,),
+        [(mine, VMEM), (theirs, VMEM), (table["left_t"], VMEM), (table["right_t"], VMEM)],
+        [((ROWS, COLS), f32, VMEM)],
         name="update",
+        held=[(ROWS, COLS)],
         **order,
     )
 
@@ -349,54 +341,39 @@
     )
 
 
-def both_kernel(own_ref, other_ref, out_ref):
+def pair_kernel(own_ref, opposite_ref, left_ref, right_ref, own_out, pair_ref):
+    own = own_ref[...] + opposite_ref[...]
+    other = left_ref[...] + right_ref[...]
+    own_out[...] = own
     is_first = lax.axis_index("fsdp") < 4
-    own, other = own_ref[...], other_ref[...]
-    out_ref[:TILE_ROWS] = jnp.where(is_first, own, other)
-    out_ref[TILE_ROWS:] = jnp.where(is_first, other, own)
-
-
-def both_of(own, other, **order):
-    return call(
-        both_kernel,
-        [(own, VMEM), (other, VMEM)],
-        [((2 * TILE_ROWS, HALF), f32, VMEM)],
-        name="both",
-        **order,
-    )
-
-
-def pair_kernel(one_ref, two_ref, own_ref, pair_ref):
-    total = one_ref[...] + two_ref[...]
-    is_first = lax.axis_index("fsdp") < 4
-    own_ref[...] = jnp.where(is_first, total[:TILE_ROWS], total[TILE_ROWS:])
-    pair_ref[...] = total.astype(bf16)
-
-
-def pair_of(one, two, **order):
+    pair_ref[:TILE_ROWS] = jnp.where(is_first, own, other).astype(bf16)
+    pair_ref[TILE_ROWS:] = jnp.where(is_first, other, own).astype(bf16)
+
+
+def pair_of(own, opposite, left, right, **order):
     return call(
         pair_kernel,
-        [(one, VMEM), (two, VMEM)],
+        [(part, VMEM) for part in (own, opposite, left, right)],
         [((TILE_ROWS, HALF), f32, VMEM), ((2 * TILE_ROWS, HALF), bf16, VMEM)],
         name="pair",
         **order,
     )
 
 
-def quad_kernel(pair_ref, other_ref, out_ref):
-    is_even = lax.rem(lax.axis_index("fsdp"), 2) == 0
-    rows = 2 * TILE_ROWS
-    pair, other = pair_ref[...], other_ref[...]
-    out_ref[:rows] = jnp.where(is_even, pair, other)
-    out_ref[rows:] = jnp.where(is_even, other, pair)
-
-
-def quad_of(pair, other, **order):
-    return call(
-        quad_kernel,
-        [(pair, VMEM), (other, VMEM)],
-        [((4 * TILE_ROWS, HALF), bf16, VMEM)],
-        name="quad",
+def pack_kernel(*refs):
+    row = 0
+    for ref in refs[:-1]:
+        refs[-1][row : row + ref.shape[0]] = ref[...]
+        row += ref.shape[0]
+
+
+def pack(arrays, name, **order):
+    shape = (sum(array.shape[0] for array in arrays), arrays[0].shape[1])
+    return call(
+        pack_kernel,
+        [(array, VMEM) for array in arrays],
+        [(shape, arrays[0].dtype, VMEM)],
+        name=name,
         **order,
     )
 
@@ -409,29 +386,30 @@
     return call(hand_on_kernel, [], [], name=name, after=after, through=arrays)[1:]
 
 
-def change_kernel(high_ref, low_ref, here_ref, there_ref, s_here_ref, s_there_ref, out_ref):
-    is_first = core_of() == 0
-    is_low = lax.rem(lax.axis_index("fsdp"), 4) < 2
-    here = here_ref[...], s_here_ref[...]
-    there = there_ref[...], s_there_ref[...]
+def change_kernel(high_ref, low_ref, bands_ref, s_bands_ref, out_ref, total):
+    core = core_of()
+    z = lax.rem(lax.axis_index("fsdp"), 4)
+    for k, side in enumerate((0, 3, 1, 2)):
+        source = lax.rem(z + side, 4)
+        for x in range(2):
+            row = pl.multiple_of((x * 4 + source) * TILE_ROWS, 16)
+            rows = slice((2 * k + x) * TILE_ROWS, (2 * k + x + 1) * TILE_ROWS)
+            total[core, pl.ds(row, TILE_ROWS)] = bands_ref[rows]
+            total[1 - core, pl.ds(row, TILE_ROWS)] = s_bands_ref[rows]
     for half in range(2):
-        near = jnp.where(is_first, here[half], here[1 - half])
-        far = jnp.where(is_first, there[half], there[1 - half])
-        one, two = jnp.where(is_low, near, far), jnp.where(is_low, far, near)
-        blocks = [part[k * TILE_ROWS : (k + 1) * TILE_ROWS] for part in (one, two) for k in range(4)]
-        total = jnp.concatenate([blocks[2 * z + x] for x in range(2) for z in range(4)], axis=0)
-        value = dot(high_ref[...], total) + dot(low_ref[...], total)
+        value = dot(high_ref[...], total[half]) + dot(low_ref[...], total[half])
         for k in range(5):
             high, low = split(value[:, k * 64 : (k + 1) * 64])
             start = (half * 5 + k) * 256
             out_ref[:, start : start + 256] = jnp.concatenate([high, low, high, low], axis=1)
 
 
-def change_of(high, low, quads, **order):
+def change_of(high, low, bands, s_bands, **order):
     return call(
         change_kernel,
-        [(array, VMEM) for array in (high, low, *quads)],
+        [(array, VMEM) for array in (high, low, bands, s_bands)],
         [((TOKENS, COLS), bf16, VMEM)],
+        scratch=[pltpu.VMEM((2, BANDS, HALF), bf16)],
         name="change",
         **order,
     )
@@ -455,48 +433,91 @@
     return [jnp.where(is_first, a, b), jnp.where(is_first, b, a)]
 
 
-def own_kernel(x_ref, w_ref, z0, sz0, z1, sz1, z2, sz2, out_ref):
+def part_of(ref, start, rows=HALF_ROWS):
+    return ref.at[pl.ds(start, rows)]
+
+
+def own_kernel(x_ref, w_ref, z0, sz0, z1, z2, s_pack, held_ref, out_ref, final_ref, sem):
     core = core_of()
+    flush = pltpu.make_async_copy(held_ref, final_ref, sem)
+    flush.start()
+    sz1, sz2 = part_of(s_pack, 0), part_of(s_pack, HALF_ROWS)
     for n in range(N_BLOCKS):
         columns = slice(n * BLOCK, (n + 1) * BLOCK)
         before, behind = beside(core, z0, sz0, z1, sz1, columns)
         rows = before + [w_ref[:, columns]] + behind + in_order(core, z2, sz2, columns)
         out_ref[:, columns] = dot(x_ref[:, : 4 * ROWS], jnp.concatenate(rows, axis=0))
-
-
-def own_product(turned, pieces, **order):
+    flush.wait()
+
+
+def own_product(turned, pieces, held, **order):
     return call(
         own_kernel,
-        [(array, VMEM) for array in (turned, *pieces)],
+        [(array, VMEM) for array in (turned, *pieces, held)],
+        [((TOKENS, COLS), f32, VMEM), (held.shape, f32, ANY)],
+        scratch=[pltpu.SemaphoreType.DMA],
+        name="own_product",
+        **order,
+    )
+
+
+def near_kernel(x_ref, acc_ref, change_ref, step_ref, x0, z0, z1, s_pack, sz1, out_ref):
+    core = core_of()
+    sz0, sx0 = part_of(s_pack, 2 * HALF_ROWS), part_of(s_pack, 3 * HALF_ROWS)
+    for n in range(N_BLOCKS):
+        columns = slice(n * BLOCK, (n + 1) * BLOCK)
+        before, behind = beside(core, z0, sz0, z1, sz1, columns)
+        rows = before + in_order(core, x0, sx0, columns) + behind
+        value = dot(x_ref[:, 4 * ROWS : 7 * ROWS], jnp.concatenate(rows, axis=0))
+        change = change_ref[:, columns]
+        steps = [dot(change[:, k : k + 256], step_ref[...]) for k in (0, 256)]
+        out_ref[:, columns] = acc_ref[:, columns] + value + jnp.concatenate(steps, axis=1)
+
+
+def near_product(turned, acc, change, pieces, table, **order):
+    return call(
+        near_kernel,
+        [(array, VMEM) for array in (turned, acc, change, table["step"], *pieces)],
         [((TOKENS, COLS), f32, VMEM)],
-        name="own_product",
-        **order,
-    )
-
-
-def rest_kernel(
-    x_ref, acc_ref, change_ref, step_ref,
-    x0, sx0, z0, sz0, z1, sz1, top, s_top, low, s_low, out_ref,
+        name="near_product",
+        **order,
+    )
+
+
+def far_kernel(
+    x_ref, acc_ref, top, low, s_last, held_ref,
+    out_ref, final_ref, result, sems,
 ):
     core = core_of()
-    columns = pl.ds(pl.multiple_of(pl.program_id(0) * BLOCK, BLOCK), BLOCK)
-    before, behind = beside(core, z0, sz0, z1, sz1, columns)
-    tops, lows = in_order(core, top, s_top, columns), in_order(core, low, s_low, columns)
-    rows = before + in_order(core, x0, sx0, columns) + behind
-    rows += [tops[0], lows[0], tops[1], lows[1]]
-    change = change_ref[:, columns]
-    steps = [dot(change[:, k : k + 256], step_ref[...]) for k in (0, 256)]
-    value = dot(x_ref[:, 4 * ROWS :], jnp.concatenate(rows, axis=0))
-    out_ref[0] = (acc_ref[:, columns] + value + jnp.concatenate(steps, axis=1)).astype(bf16)
-
-
-def rest_product(turned, acc, change, pieces, table, **order):
-    return call(
-        rest_kernel,
-        [(array, VMEM) for array in (turned, acc, change, table["step"], *pieces)],
-        [((1, TOKENS, COLS), bf16, column_block_of_one(TOKENS, BLOCK))],
-        grid=(N_BLOCKS,),
-        name="rest_product",
+    s_top, s_low = part_of(s_last, 0, QUARTER), part_of(s_last, QUARTER, QUARTER)
+    flush = pltpu.make_async_copy(held_ref, final_ref, sems.at[N_BLOCKS])
+    flush.start()
+
+    def write(n):
+        columns = pl.ds(n * BLOCK, BLOCK)
+        return pltpu.make_async_copy(
+            result.at[:, columns], out_ref.at[0, :, columns], sems.at[n]
+        )
+
+    for n in range(N_BLOCKS):
+        columns = slice(n * BLOCK, (n + 1) * BLOCK)
+        tops, lows = in_order(core, top, s_top, columns), in_order(core, low, s_low, columns)
+        rows = jnp.concatenate([tops[0], lows[0], tops[1], lows[1]], axis=0)
+        value = dot(x_ref[:, 7 * ROWS :], rows)
+        result[:, columns] = (acc_ref[:, columns] + value).astype(bf16)
+        write(n).start()
+    for n in range(N_BLOCKS):
+        write(n).wait()
+    flush.wait()
+
+
+def far_product(turned, acc, pieces, held, **order):
+    return call(
+        far_kernel,
+        [(array, VMEM) for array in (turned, acc, *pieces, held)],
+        [((1, TOKENS, COLS), bf16, ANY), (held.shape, f32, ANY)],
+        scratch=[pltpu.VMEM((TOKENS, COLS), bf16), pltpu.SemaphoreType.DMA((N_BLOCKS + 1,))],
+        name="far_product",
         **order,
     )
 
@@ -536,37 +557,31 @@
     xz0 = along_x(z0)
     z2 = along_z(z0)
     sz0 = across(z0)
-    column, _, z1, sz0, x0 = sum_of([half_sum, rest_y], "y_sum", through=[z1, sz0, x0])
-    half_x = swapped(column, 0, 0)
+    column, _, z1, sz0 = sum_of([half_sum, rest_y], "y_sum", through=[z1, sz0])
+    x_parts = by(column, 0, 2), by(column, 0, 1), by(column, 0, -1)
+    new_momentum, done = momentum_less_band(moment, coeffs, table, after=[column])
+    own, pair, _, xz0, z2 = pair_of(column, *x_parts, after=[done], through=[xz0, z2])
+    z_parts = by(pair, 2, 1), by(pair, 2, -1), by(pair, 2, 2)
     xz1 = along_x(z1)
-    sz1 = across(z1)
-    both, _, xz0, z2, x0, sz1 = both_of(column, half_x, through=[xz0, z2, x0, sz1])
-    rest_x = swapped(both, 0, 1)
-    sx0, sz2, sxz0 = across(x0), across(z2), across(xz0)
-    new_momentum, done = momentum_less_band(moment, coeffs, table, after=[both])
-    own, pair, _, xz1, sx0, sz2, sxz0, z2, xz0 = pair_of(
-        both, rest_x, after=[done], through=[xz1, sx0, sz2, sxz0, z2, xz0]
-    )
-    half_z = swapped(pair, 2, 0)
-    s_own, sxz1 = across(own), across(xz1)
+    near, done = pack([z1, z2, xz0, x0], "pack_near", after=[pair])
+    s_near = across(near)
+    acc, new_momentum, done = own_product(
+        turned, [weights, z0, sz0, z1, z2, s_near], new_momentum, after=[done]
+    )
+    bands, done = pack([pair, *z_parts], "pack_bands", after=[done])
+    s_bands = across(bands)
     xz2 = along_x(z2[:QUARTER])
     z3 = along_z(xz0[QUARTER:])
-    update, done = update_of(own, s_own, table, after=[pair])
-    quad, _, sxz1 = quad_of(pair, half_z, after=[done], through=[sxz1])
-    rest_z = swapped(quad, 2, 1)
-    s_quad = across(quad)
-    acc, done, s_quad = own_product(
-        turned, [weights, z0, sz0, z1, sz1, z2, sz2], after=[quad], through=[s_quad]
-    )
-    rest_z, xz2, z3 = hand_on([rest_z, xz2, z3], [done], "after_own_product")
-    change, _ = change_of(high, low, [quad, rest_z, s_quad, across(rest_z)])
-    result, _ = rest_product(
-        turned,
-        acc,
-        change,
-        [x0, sx0, xz0, sxz0, xz1, sxz1, xz2, across(xz2), z3, across(z3)],
-        table,
-    )
+    xz1, own = hand_on([xz1, own], [done], "after_pack_bands")
+    sxz1, s_own = across(xz1), across(own)
+    change, done = change_of(high, low, bands, s_bands, after=[own])
+    acc, done, s_own = near_product(
+        turned, acc, change, [x0, xz0, xz1, s_near, sxz1], table, after=[done], through=[s_own]
+    )
+    last, done = pack([xz2, z3], "pack_last", after=[done])
+    s_last = across(last)
+    update, done = update_of(own, s_own, table, after=[done])
+    result, update, _ = far_product(turned, acc, [xz2, z3, s_last], update, after=[done])
     return (new_momentum, update, result)
 
 

time: 88.8 us -> 75.3 us (0.85)
  waiting for transfers between devices: 19.1 us -> 12.9 us
  Pallas kernels: 36.8 us -> 31.9 us
  starting transfers between devices: 31.9 us -> 29.3 us
    ppermute x6 -> x2, starting transfers between devices: 11.2 us -> 4.03 us  [swapped(): return lax.ppermute(value, BOTH, pairs)]
    ppermute x6 -> x2, waiting for transfers between devices: 7.74 us -> 1.34 us  [swapped(): return lax.ppermute(value, BOTH, pairs)]
    pallas_call x14 -> x16, Pallas kernels: 36.8 us -> 31.9 us  [call(): pl.pallas_call(body, grid=grid, out_shape=tuple((pltpu.VMEM(shape, dtype)...]
    ppermute x20 -> x21, starting transfers between devices: 20.7 us -> 25.2 us  [moved(): return lax.ppermute(value, BOTH, pairs)]
    ppermute x20 -> x21, waiting for transfers between devices: 11.4 us -> 11.5 us  [moved(): return lax.ppermute(value, BOTH, pairs)]
  transfers between devices with their start and end apart: 26 -> 23, of which waited for: 11 -> 10; matrix products, arithmetic and copies ran while one was open for 0% -> 0% of each run, Pallas kernels for 27% -> 30%
where the time goes in v2:
time: 75.3 us; the launch traced here: 75.1 us
  Pallas kernels  31.9 us (42%)
  starting transfers between devices  29.3 us (39%)
  waiting for transfers between devices  12.9 us (17%)
  between operations  0.99 us (1%)
    pallas_call x16, Pallas kernels, call(): pl.pallas_call(body, grid=grid, out_shape=tuple((pltpu.VMEM(shape, dtype)...  31.9 us
    ppermute x21, starting transfers between devices, moved(): return lax.ppermute(value, BOTH, pairs)  25.2 us
    ppermute x21, waiting for transfers between devices, moved(): return lax.ppermute(value, BOTH, pairs)  11.5 us
    ppermute x2, starting transfers between devices, swapped(): return lax.ppermute(value, BOTH, pairs)  4.03 us
  transfers between devices with their start and end apart: 23, of which 10 were waited for; matrix products, arithmetic and copies ran while one was open for 0% of the time, Pallas kernels for 30%

profile of v2, /device:TPU:1, one launch (start us, length us, event | category | flops | bytes accessed | tf_op | source)
XLA Modules:
  0.0 75.1 jit_solution(18305527705696241611)
XLA Ops:
  0.6 4.7 %band.1 = (f32[80,640]{1,0:T(8,128)S(1)}, f32[80,320]{1,0:T(8,128)S(1)}, f32[80,320]{1,0:T(8,128)S(1)}, f32[320,2560]{1,0:T(8,128)S(1)}, bf16[160,2560]{1,0:T(8,...) custom-call(f32[1,320,2560]{2,1,0:T(8,128)} %refs_0_.2, bf16[1,320,2560]{2,1,0:T(8,128)(2,1)} %refs_1_.3, ...), custom_call_target="tpu_custom_call" | custom-call | flops 1 | bytes 1 | tf_op jit(solution)/shard_map/band/pallas_call | solution.py:125
  5.3 3.4 %collective-permute-start.3 = (bf16[160,2560]{1,0:T(8,128)(2,1)S(1)}, bf16[160,2560]{1,0:T(8,128)(2,1)S(1)}, u32[]{:S(2)}, u32[]{:S(2)}) collective-permute-start(bf16[160,2560]{1,0:T(8,128)(2,1)S(1)} %get-tuple-element.51), channel_id=1, source_target_pairs={{0,4},{1,5},{2,6},{3,7},{4,16},{5,17},{6,18},{7,19},{8,28},{9,29},... | collective-permute-start | bytes 2457608 | tf_op jit(solution)/shard_map/ppermute | solution.py:42
  8.7 3.8 %collective-permute-start.2 = (bf16[160,2560]{1,0:T(8,128)(2,1)S(1)}, bf16[160,2560]{1,0:T(8,128)(2,1)S(1)}, u32[]{:S(2)}, u32[]{:S(2)}) collective-permute-start(bf16[160,2560]{1,0:T(8,128)(2,1)S(1)} %get-tuple-element.51), channel_id=1, source_target_pairs={{0,1},{1,2},{2,3},{3,0},{4,5},{5,6},{6,7},{7,4},{8,11},{9,8},{10,9... | collective-permute-start | bytes 2457608 | tf_op jit(solution)/shard_map/ppermute | solution.py:42
  12.5 0.0 collective-permute-start
  12.5 1.3 %collective-permute-done.refs_1_ = f32[80,320]{1,0:T(8,128)S(1)} collective-permute-done((f32[80,320]{1,0:T(8,128)S(1)}, f32[80,320]{1,0:T(8,128)S(1)}, u32[]{:S(2)}, u32[]{:S(2)}) %collective-permute-start) | collective-permute-done | bytes 102432 | tf_op jit(solution)/shard_map/ppermute | solution.py:42
  13.8 0.6 chip_sum.1
  14.4 1.3 %collective-permute-start.1 = (f32[80,320]{1,0:T(8,128)S(1)}, f32[80,320]{1,0:T(8,128)S(1)}, u32[]{:S(2)}, u32[]{:S(2)}) collective-permute-start(f32[80,320]{1,0:T(8,128)S(1)} %get-tuple-element.48.refs_2_.refs_0_), channel_id=1, source_target_pairs={{0,32},{1,33},{2,34},{3,35},{4,36},{5,37},{6,38},{7,39},{8,40},{9,... | collective-permute-start | bytes 307208 | tf_op jit(solution)/shard_map/ppermute | solution.py:531
  15.7 0.1 collective-permute-start.5
  15.8 4.5 %input_band.1 = (bf16[640,640]{1,0:T(8,128)(2,1)S(1)}, bf16[640,640]{1,0:T(8,128)(2,1)S(1)}, bf16[640,2560]{1,0:T(8,128)(2,1)S(1)}, f32[8,128]{1,0:T(8,128)S(1)}) custom-call(bf16[1,640,2560]{2,1,0:T(8,128)(2,1)} %refs_0_.3, bf16[512,256]{1,0:T(8,128)(2,1)} %constant.14.clone.refs_1_, f32[80,320]{1,0:T(8,128)S(1)} %get-tuple-element.48.refs_2_.refs_0_), custom_call_target="tpu_custom_call" | custom-call | flops 1 | bytes 1 | tf_op jit(solution)/shard_map/input_band/pallas_call | solution.py:125
  20.4 0.0 collective-permute-done.1.refs_1_
  20.4 0.0 collective-permute-done.3.refs_4_
  20.4 1.4 %collective-permute-done.2.refs_3_ = bf16[160,2560]{1,0:T(8,128)(2,1)S(1)} collective-permute-done((bf16[160,2560]{1,0:T(8,128)(2,1)S(1)}, bf16[160,2560]{1,0:T(8,128)(2,1)S(1)}, u32[]{:S(2)}, u32[]{:S(2)}) %collective-permute-start.2) | collective-permute-done | bytes 819232 | tf_op jit(solution)/shard_map/ppermute | solution.py:42
  21.7 0.6 half_y_sum.1
  22.4 1.0 %collective-permute-start.6 = (bf16[160,2560]{1,0:T(8,128)(2,1)S(1)}, bf16[160,2560]{1,0:T(8,128)(2,1)S(1)}, u32[]{:S(2)}, u32[]{:S(2)}) collective-permute-start(bf16[160,2560]{1,0:T(8,128)(2,1)S(1)} %get-tuple-element.52.refs_2_), channel_id=1, source_target_pairs={{0,8},{1,9},{2,10},{3,11},{4,12},{5,13},{6,14},{7,15},{8,0},{9,1},... | collective-permute-start | bytes 2457608 | tf_op jit(solution)/shard_map/ppermute | solution.py:42
  23.3 2.1 %collective-permute-start.11 = (bf16[160,2560]{1,0:T(8,128)(2,1)S(1)}, bf16[160,2560]{1,0:T(8,128)(2,1)S(1)}, u32[]{:S(2)}, u32[]{:S(2)}) collective-permute-start(bf16[160,2560]{1,0:T(8,128)(2,1)S(1)} %get-tuple-element.52.refs_2_), channel_id=1, source_target_pairs={{0,1},{1,2},{2,3},{3,0},{4,5},{5,6},{6,7},{7,4},{8,11},{9,8},{10,9... | collective-permute-start | bytes 2457608 | tf_op jit(solution)/shard_map/ppermute | solution.py:42
  25.5 1.1 %collective-permute-start.10 = (bf16[160,2560]{1,0:T(8,128)(2,1)S(1)}, bf16[160,2560]{1,0:T(8,128)(2,1)S(1)}, u32[]{:S(2)}, u32[]{:S(2)}) collective-permute-start(bf16[160,2560]{1,0:T(8,128)(2,1)S(1)} %get-tuple-element.52.refs_2_), channel_id=1, source_target_pairs={{0,4},{1,5},{2,6},{3,7},{4,16},{5,17},{6,18},{7,19},{8,28},{9,29},... | collective-permute-start | bytes 2457608 | tf_op jit(solution)/shard_map/ppermute | solution.py:42
  26.6 2.7 %collective-permute-start.4 = (f32[80,320]{1,0:T(8,128)S(1)}, f32[80,320]{1,0:T(8,128)S(1)}, u32[]{:S(2)}, u32[]{:S(2)}) collective-permute-start(f32[80,320]{1,0:T(8,128)S(1)} %get-tuple-element.53.refs_0_), channel_id=1, source_target_pairs={{0,96},{1,97},{2,98},{3,99},{4,100},{5,101},{6,102},{7,103},{8,104... | collective-permute-start | bytes 307208 | tf_op jit(solution)/shard_map/ppermute | solution.py:531
  29.3 1.2 %collective-permute-done.5.refs_2_ = bf16[160,2560]{1,0:T(8,128)(2,1)S(1)} collective-permute-done((bf16[160,2560]{1,0:T(8,128)(2,1)S(1)}, bf16[160,2560]{1,0:T(8,128)(2,1)S(1)}, u32[]{:S(2)}, u32[]{:S(2)}) %collective-permute-start.5) | collective-permute-done | bytes 819232 | tf_op jit(solution)/shard_map/ppermute | solution.py:42
  30.5 1.3 %collective-permute-done.4.refs_1_ = f32[80,320]{1,0:T(8,128)S(1)} collective-permute-done((f32[80,320]{1,0:T(8,128)S(1)}, f32[80,320]{1,0:T(8,128)S(1)}, u32[]{:S(2)}, u32[]{:S(2)}) %collective-permute-start.4) | collective-permute-done | bytes 102432 | tf_op jit(solution)/shard_map/ppermute | solution.py:531
  31.9 0.0 collective-permute-done.6.refs_3_
  31.9 0.6 y_sum.1
  32.5 1.5 %collective-permute-start.9 = (f32[80,320]{1,0:T(8,128)S(1)}, f32[80,320]{1,0:T(8,128)S(1)}, u32[]{:S(2)}, u32[]{:S(2)}) collective-permute-start(f32[80,320]{1,0:T(8,128)S(1)} %get-tuple-element.57.refs_4_.refs_0_), channel_id=1, source_target_pairs={{0,20},{1,21},{2,22},{3,23},{4,0},{5,1},{6,2},{7,3},{8,28},{9,29},... | collective-permute-start | bytes 307208 | tf_op jit(solution)/shard_map/ppermute | solution.py:42
  34.0 0.0 collective-permute-start.8
  34.0 1.5 %collective-permute-start.7 = (f32[80,320]{1,0:T(8,128)S(1)}, f32[80,320]{1,0:T(8,128)S(1)}, u32[]{:S(2)}, u32[]{:S(2)}) collective-permute-start(f32[80,320]{1,0:T(8,128)S(1)} %get-tuple-element.57.refs_4_.refs_0_), channel_id=1, source_target_pairs={{0,16},{1,17},{2,18},{3,19},{4,20},{5,21},{6,22},{7,23},{8,24},{9,... | collective-permute-start | bytes 307208 | tf_op jit(solution)/shard_map/ppermute | solution.py:42
  35.5 0.0 copy-done
  35.5 0.0 copy-done.1
  35.5 1.6 %momentum_less_band.1 = (f32[1,320,2560]{2,1,0:T(8,128)S(1)}, f32[8,128]{1,0:T(8,128)S(1)}) custom-call(f32[320,2560]{1,0:T(8,128)S(1)} %get-tuple-element.58.refs_0_, f32[80,640]{1,0:T(8,128)S(1)} %get-tuple-element.59.refs_1_, bf16[320,240]{1,0:T(8,128)(2,1)S(1)} %copy-done.1, bf16[384,512]{1,0:T(8,128)(2,1)S(1)} %copy-done, ...), custom_call_target="tpu_custom_call" | custom-call | flops 1 | bytes 1 | tf_op jit(solution)/shard_map/momentum_less_band/pallas_call | solution.py:125
  37.1 2.2 %collective-permute-done.11.refs_6_ = bf16[160,2560]{1,0:T(8,128)(2,1)S(1)} collective-permute-done((bf16[160,2560]{1,0:T(8,128)(2,1)S(1)}, bf16[160,2560]{1,0:T(8,128)(2,1)S(1)}, u32[]{:S(2)}, u32[]{:S(2)}) %collective-permute-start.11) | collective-permute-done | bytes 819232 | tf_op jit(solution)/shard_map/ppermute | solution.py:42
  39.3 0.0 collective-permute-done.10.refs_5_
  39.3 0.7 collective-permute-done.9.refs_3_
  40.0 2.8 %collective-permute-done.8.refs_2_ = f32[80,320]{1,0:T(8,128)S(1)} collective-permute-done((f32[80,320]{1,0:T(8,128)S(1)}, f32[80,320]{1,0:T(8,128)S(1)}, u32[]{:S(2)}, u32[]{:S(2)}) %collective-permute-start.8) | collective-permute-done | bytes 102432 | tf_op jit(solution)/shard_map/ppermute | solution.py:42
  42.8 0.0 collective-permute-done.7.refs_1_
  42.8 0.6 pair.1
  43.5 0.2 pack_near.1
  43.7 0.8 %collective-permute-start.12 = (bf16[640,2560]{1,0:T(8,128)(2,1)S(1)}, bf16[640,2560]{1,0:T(8,128)(2,1)S(1)}, u32[]{:S(2)}, u32[]{:S(2)}) collective-permute-start(bf16[640,2560]{1,0:T(8,128)(2,1)S(1)} %get-tuple-element.65), channel_id=1, source_target_pairs={{0,8},{1,9},{2,10},{3,11},{4,12},{5,13},{6,14},{7,15},{8,0},{9,1},... | collective-permute-start | bytes 9830408 | tf_op jit(solution)/shard_map/ppermute | solution.py:42
  44.5 1.0 %collective-permute-start.17 = (bf16[160,2560]{1,0:T(8,128)(2,1)S(1)}, bf16[160,2560]{1,0:T(8,128)(2,1)S(1)}, u32[]{:S(2)}, u32[]{:S(2)}) collective-permute-start(bf16[160,2560]{1,0:T(8,128)(2,1)S(1)} %get-tuple-element.56.refs_0_.refs_4_), channel_id=1, source_target_pairs={{0,4},{1,5},{2,6},{3,7},{4,16},{5,17},{6,18},{7,19},{8,28},{9,29},... | collective-permute-start | bytes 2457608 | tf_op jit(solution)/shard_map/ppermute | solution.py:42
  45.5 2.1 %collective-permute-start.15 = (bf16[160,320]{1,0:T(8,128)(2,1)S(1)}, bf16[160,320]{1,0:T(8,128)(2,1)S(1)}, u32[]{:S(2)}, u32[]{:S(2)}) collective-permute-start(bf16[160,320]{1,0:T(8,128)(2,1)S(1)} %get-tuple-element.64.refs_4_.refs_0_), channel_id=1, source_target_pairs={{0,2},{1,3},{2,0},{3,1},{4,6},{5,7},{6,4},{7,5},{8,10},{9,11},{10,... | collective-permute-start | bytes 307208 | tf_op jit(solution)/shard_map/ppermute | solution.py:42
  47.7 0.5 collective-permute-start.14
  48.1 1.0 %collective-permute-start.13 = (bf16[160,320]{1,0:T(8,128)(2,1)S(1)}, bf16[160,320]{1,0:T(8,128)(2,1)S(1)}, u32[]{:S(2)}, u32[]{:S(2)}) collective-permute-start(bf16[160,320]{1,0:T(8,128)(2,1)S(1)} %get-tuple-element.64.refs_4_.refs_0_), channel_id=1, source_target_pairs={{0,1},{1,2},{2,3},{3,0},{4,5},{5,6},{6,7},{7,4},{8,9},{9,10},{10,1... | collective-permute-start | bytes 307208 | tf_op jit(solution)/shard_map/ppermute | solution.py:42
  49.1 0.8 %collective-permute-done.12.refs_6_.refs_7_ = bf16[640,2560]{1,0:T(8,128)(2,1)S(1)} collective-permute-done((bf16[640,2560]{1,0:T(8,128)(2,1)S(1)}, bf16[640,2560]{1,0:T(8,128)(2,1)S(1)}, u32[]{:S(2)}, u32[]{:S(2)}) %collective-permute-start.12) | collective-permute-done | bytes 3276832 | tf_op jit(solution)/shard_map/ppermute | solution.py:42
  50.0 5.9 %own_product.1 = (f32[640,2560]{1,0:T(8,128)S(1)}, f32[1,320,2560]{2,1,0:T(8,128)}, f32[8,128]{1,0:T(8,128)S(1)}) custom-call(bf16[640,2560]{1,0:T(8,128)(2,1)S(1)} %get-tuple-element.49.refs_0_, bf16[320,2560]{1,0:T(8,128)(2,1)} %refs_1_.4, bf16[160,2560]{1,0:T(8,128)(2,1)S(1)} %get-tuple-element.52.refs_2_, ...), custom_call_target="tpu_custom_call" | custom-call | flops 1 | bytes 1 | tf_op jit(solution)/shard_map/own_product/pallas_call | solution.py:125
  55.9 0.0 copy-start.2
  55.9 0.0 collective-permute-done.15.refs_3_
  55.9 0.0 collective-permute-done.14.refs_2_
  55.9 0.0 collective-permute-done.13.refs_1_
  56.0 0.0 collective-permute-done.17.refs_1_
  56.0 0.6 after_pack_bands.1
  56.6 2.1 %collective-permute-start.18 = (bf16[160,2560]{1,0:T(8,128)(2,1)S(1)}, bf16[160,2560]{1,0:T(8,128)(2,1)S(1)}, u32[]{:S(2)}, u32[]{:S(2)}) collective-permute-start(bf16[160,2560]{1,0:T(8,128)(2,1)S(1)} %get-tuple-element.78.refs_6_), channel_id=1, source_target_pairs={{0,8},{1,9},{2,10},{3,11},{4,12},{5,13},{6,14},{7,15},{8,0},{9,1},... | collective-permute-start | bytes 2457608 | tf_op jit(solution)/shard_map/ppermute | solution.py:42
  58.7 0.0 collective-permute-start.16
  58.8 1.6 %collective-permute-start.21 = (bf16[80,2560]{1,0:T(8,128)(2,1)S(1)}, bf16[80,2560]{1,0:T(8,128)(2,1)S(1)}, u32[]{:S(2)}, u32[]{:S(2)}) collective-permute-start(bf16[80,2560]{1,0:T(8,128)(2,1)S(1)} %slice.7), channel_id=1, source_target_pairs={{0,1},{1,2},{2,3},{3,0},{4,5},{5,6},{6,7},{7,4},{8,11},{9,8},{10,9... | collective-permute-start | bytes 1228808 | tf_op jit(solution)/shard_map/ppermute | solution.py:42
  60.4 0.4 collective-permute-start.20
  60.8 0.0 collective-permute-start.19
  60.8 0.6 collective-permute-done.16.refs_3_
  61.4 2.3 %change.1 = (bf16[640,2560]{1,0:T(8,128)(2,1)S(1)}, f32[8,128]{1,0:T(8,128)S(1)}) custom-call(bf16[640,640]{1,0:T(8,128)(2,1)S(1)} %get-tuple-element.70.refs_0_, bf16[640,640]{1,0:T(8,128)(2,1)S(1)} %get-tuple-element.71.refs_1_, bf16[640,320]{1,0:T(8,128)(2,1)S(1)} %get-tuple-element.73.refs_2_, bf16[640,320]{1,0:T(8,128)(2,1)S(1)} %collective-permute-done.16.refs_3_, ...), custom_call_target="tpu_custom_call" | custom-call | flops 1 | bytes 1 | tf_op jit(solution)/shard_map/change/pallas_call | solution.py:125
  63.7 0.0 collective-permute-done.19.refs_10_
  63.7 0.0 collective-permute-done.18.refs_8_
  63.7 4.5 %near_product.1 = (f32[640,2560]{1,0:T(8,128)S(1)}, f32[8,128]{1,0:T(8,128)S(1)}, f32[80,320]{1,0:T(8,128)S(1)}) custom-call(bf16[640,2560]{1,0:T(8,128)(2,1)S(1)} %get-tuple-element.49.refs_0_, f32[640,2560]{1,0:T(8,128)S(1)} %get-tuple-element.69.refs_1_, bf16[640,2560]{1,0:T(8,128)(2,1)S(1)} %get-tuple-element.77.refs_2_, ...), custom_call_target="tpu_custom_call", output_to_operand_aliasing={{2}: (10, {})} | custom-call | flops 1 | bytes 1 | tf_op jit(solution)/shard_map/near_product/pallas_call | solution.py:125
  68.2 0.0 collective-permute-done.21.refs_1_.refs_3_
  68.2 0.0 collective-permute-done.20.refs_0_.refs_2_
  68.2 0.1 pack_last.1
  68.3 1.2 %collective-permute-start.22 = (bf16[160,2560]{1,0:T(8,128)(2,1)S(1)}, bf16[160,2560]{1,0:T(8,128)(2,1)S(1)}, u32[]{:S(2)}, u32[]{:S(2)}) collective-permute-start(bf16[160,2560]{1,0:T(8,128)(2,1)S(1)} %get-tuple-element.82), channel_id=1, source_target_pairs={{0,8},{1,9},{2,10},{3,11},{4,12},{5,13},{6,14},{7,15},{8,0},{9,1},... | collective-permute-start | bytes 2457608 | tf_op jit(solution)/shard_map/ppermute | solution.py:42
  69.5 1.6 %update.1 = (f32[320,2560]{1,0:T(8,128)S(1)}, f32[8,128]{1,0:T(8,128)S(1)}) custom-call(f32[80,320]{1,0:T(8,128)S(1)} %get-tuple-element.76.refs_4_.refs_0_, f32[80,320]{1,0:T(8,128)S(1)} %get-tuple-element.83.refs_1_, bf16[320,240]{1,0:T(8,128)(2,1)S(1)} %copy-done.1, bf16[384,512]{1,0:T(8,128)(2,1)S(1)} %copy-done, f32[8,128]{1,0:T(8,128)S(1)} %get-tuple-element.84.refs_4_), custom_call_target="tpu_custom_call" | custom-call | flops 1 | bytes 1 | tf_op jit(solution)/shard_map/update/pallas_call | solution.py:125
  71.1 0.4 collective-permute-done.22.refs_4_
  71.5 3.5 %far_product.1 = (bf16[1,640,2560]{2,1,0:T(8,128)(2,1)}, f32[320,2560]{1,0:T(8,128)}, f32[8,128]{1,0:T(8,128)}) custom-call(bf16[640,2560]{1,0:T(8,128)(2,1)S(1)} %get-tuple-element.49.refs_0_, f32[640,2560]{1,0:T(8,128)S(1)} %get-tuple-element.80.refs_1_, bf16[80,2560]{1,0:T(8,128)(2,1)S(1)} %collective-permute-done.20.refs_0_.refs_2_, ...), custom_call_target="tpu_custom_call" | custom-call | flops 1 | bytes 1 | tf_op jit(solution)/shard_map/far_product/pallas_call | solution.py:125
  (6 shorter events, 0.1 us)
Async XLA Ops:
  5.3 15.1 %collective-permute-start.3 = (bf16[160,2560]{1,0:T(8,128)(2,1)S(1)}, bf16[160,2560]{1,0:T(8,128)(2,1)S(1)}, u32[]{:S(2)}, u32[]{:S(2)}) collective-permute-start(bf16[160,2560]{1,0:T(8,128)(2,1)S(1)} %get-tuple-element.51), channel_id=1, source_target_pairs={{0,4},{1,5},{2,6},{3,7},{4,16},{5,17},{6,18},{7,19},{8,28},{9,29},... | collective-permute-start | bytes 2457608 | tf_op jit(solution)/shard_map/ppermute | solution.py:42
  8.7 13.0 %collective-permute-start.2 = (bf16[160,2560]{1,0:T(8,128)(2,1)S(1)}, bf16[160,2560]{1,0:T(8,128)(2,1)S(1)}, u32[]{:S(2)}, u32[]{:S(2)}) collective-permute-start(bf16[160,2560]{1,0:T(8,128)(2,1)S(1)} %get-tuple-element.51), channel_id=1, source_target_pairs={{0,1},{1,2},{2,3},{3,0},{4,5},{5,6},{6,7},{7,4},{8,11},{9,8},{10,9... | collective-permute-start | bytes 2457608 | tf_op jit(solution)/shard_map/ppermute | solution.py:42
  12.5 1.3 %collective-permute-start = (f32[80,320]{1,0:T(8,128)S(1)}, f32[80,320]{1,0:T(8,128)S(1)}, u32[]{:S(2)}, u32[]{:S(2)}) collective-permute-start(f32[80,320]{1,0:T(8,128)S(1)} %get-tuple-element.47), channel_id=1, source_target_pairs={{0,8},{1,9},{2,10},{3,11},{4,12},{5,13},{6,14},{7,15},{8,0},{9,1},... | collective-permute-start | bytes 307208 | tf_op jit(solution)/shard_map/ppermute | solution.py:42
  14.4 6.0 %collective-permute-start.1 = (f32[80,320]{1,0:T(8,128)S(1)}, f32[80,320]{1,0:T(8,128)S(1)}, u32[]{:S(2)}, u32[]{:S(2)}) collective-permute-start(f32[80,320]{1,0:T(8,128)S(1)} %get-tuple-element.48.refs_2_.refs_0_), channel_id=1, source_target_pairs={{0,32},{1,33},{2,34},{3,35},{4,36},{5,37},{6,38},{7,39},{8,40},{9,... | collective-permute-start | bytes 307208 | tf_op jit(solution)/shard_map/ppermute | solution.py:531
  15.7 19.8 %copy-start = (bf16[384,512]{1,0:T(8,128)(2,1)S(1)}, bf16[384,512]{1,0:T(8,128)(2,1)}, u32[]{:S(2)}) copy-start(bf16[384,512]{1,0:T(8,128)(2,1)} %constant.16.clone.refs_3_) | copy-start | bytes 1179652
  15.7 19.8 %copy-start.1 = (bf16[320,240]{1,0:T(8,128)(2,1)S(1)}, bf16[320,240]{1,0:T(8,128)(2,1)}, u32[]{:S(2)}) copy-start(bf16[320,240]{1,0:T(8,128)(2,1)} %constant.15.clone.refs_2_) | copy-start | bytes 460804
  15.7 14.8 %collective-permute-start.5 = (bf16[160,2560]{1,0:T(8,128)(2,1)S(1)}, bf16[160,2560]{1,0:T(8,128)(2,1)S(1)}, u32[]{:S(2)}, u32[]{:S(2)}) collective-permute-start(bf16[160,2560]{1,0:T(8,128)(2,1)S(1)} %get-tuple-element.54), channel_id=1, source_target_pairs={{0,1},{1,2},{2,3},{3,0},{4,5},{5,6},{6,7},{7,4},{8,11},{9,8},{10,9... | collective-permute-start | bytes 2457608 | tf_op jit(solution)/shard_map/ppermute | solution.py:42
  22.4 9.5 %collective-permute-start.6 = (bf16[160,2560]{1,0:T(8,128)(2,1)S(1)}, bf16[160,2560]{1,0:T(8,128)(2,1)S(1)}, u32[]{:S(2)}, u32[]{:S(2)}) collective-permute-start(bf16[160,2560]{1,0:T(8,128)(2,1)S(1)} %get-tuple-element.52.refs_2_), channel_id=1, source_target_pairs={{0,8},{1,9},{2,10},{3,11},{4,12},{5,13},{6,14},{7,15},{8,0},{9,1},... | collective-permute-start | bytes 2457608 | tf_op jit(solution)/shard_map/ppermute | solution.py:42
  23.3 16.0 %collective-permute-start.11 = (bf16[160,2560]{1,0:T(8,128)(2,1)S(1)}, bf16[160,2560]{1,0:T(8,128)(2,1)S(1)}, u32[]{:S(2)}, u32[]{:S(2)}) collective-permute-start(bf16[160,2560]{1,0:T(8,128)(2,1)S(1)} %get-tuple-element.52.refs_2_), channel_id=1, source_target_pairs={{0,1},{1,2},{2,3},{3,0},{4,5},{5,6},{6,7},{7,4},{8,11},{9,8},{10,9... | collective-permute-start | bytes 2457608 | tf_op jit(solution)/shard_map/ppermute | solution.py:42
  25.5 13.8 %collective-permute-start.10 = (bf16[160,2560]{1,0:T(8,128)(2,1)S(1)}, bf16[160,2560]{1,0:T(8,128)(2,1)S(1)}, u32[]{:S(2)}, u32[]{:S(2)}) collective-permute-start(bf16[160,2560]{1,0:T(8,128)(2,1)S(1)} %get-tuple-element.52.refs_2_), channel_id=1, source_target_pairs={{0,4},{1,5},{2,6},{3,7},{4,16},{5,17},{6,18},{7,19},{8,28},{9,29},... | collective-permute-start | bytes 2457608 | tf_op jit(solution)/shard_map/ppermute | solution.py:42
  26.6 5.3 %collective-permute-start.4 = (f32[80,320]{1,0:T(8,128)S(1)}, f32[80,320]{1,0:T(8,128)S(1)}, u32[]{:S(2)}, u32[]{:S(2)}) collective-permute-start(f32[80,320]{1,0:T(8,128)S(1)} %get-tuple-element.53.refs_0_), channel_id=1, source_target_pairs={{0,96},{1,97},{2,98},{3,99},{4,100},{5,101},{6,102},{7,103},{8,104... | collective-permute-start | bytes 307208 | tf_op jit(solution)/shard_map/ppermute | solution.py:531
  32.5 7.5 %collective-permute-start.9 = (f32[80,320]{1,0:T(8,128)S(1)}, f32[80,320]{1,0:T(8,128)S(1)}, u32[]{:S(2)}, u32[]{:S(2)}) collective-permute-start(f32[80,320]{1,0:T(8,128)S(1)} %get-tuple-element.57.refs_4_.refs_0_), channel_id=1, source_target_pairs={{0,20},{1,21},{2,22},{3,23},{4,0},{5,1},{6,2},{7,3},{8,28},{9,29},... | collective-permute-start | bytes 307208 | tf_op jit(solution)/shard_map/ppermute | solution.py:42
  34.0 8.9 %collective-permute-start.8 = (f32[80,320]{1,0:T(8,128)S(1)}, f32[80,320]{1,0:T(8,128)S(1)}, u32[]{:S(2)}, u32[]{:S(2)}) collective-permute-start(f32[80,320]{1,0:T(8,128)S(1)} %get-tuple-element.57.refs_4_.refs_0_), channel_id=1, source_target_pairs={{0,4},{1,5},{2,6},{3,7},{4,16},{5,17},{6,18},{7,19},{8,12},{9,13},... | collective-permute-start | bytes 307208 | tf_op jit(solution)/shard_map/ppermute | solution.py:42
  34.0 8.9 %collective-permute-start.7 = (f32[80,320]{1,0:T(8,128)S(1)}, f32[80,320]{1,0:T(8,128)S(1)}, u32[]{:S(2)}, u32[]{:S(2)}) collective-permute-start(f32[80,320]{1,0:T(8,128)S(1)} %get-tuple-element.57.refs_4_.refs_0_), channel_id=1, source_target_pairs={{0,16},{1,17},{2,18},{3,19},{4,20},{5,21},{6,22},{7,23},{8,24},{9,... | collective-permute-start | bytes 307208 | tf_op jit(solution)/shard_map/ppermute | solution.py:42
  43.7 6.3 %collective-permute-start.12 = (bf16[640,2560]{1,0:T(8,128)(2,1)S(1)}, bf16[640,2560]{1,0:T(8,128)(2,1)S(1)}, u32[]{:S(2)}, u32[]{:S(2)}) collective-permute-start(bf16[640,2560]{1,0:T(8,128)(2,1)S(1)} %get-tuple-element.65), channel_id=1, source_target_pairs={{0,8},{1,9},{2,10},{3,11},{4,12},{5,13},{6,14},{7,15},{8,0},{9,1},... | collective-permute-start | bytes 9830408 | tf_op jit(solution)/shard_map/ppermute | solution.py:42
  44.5 11.5 %collective-permute-start.17 = (bf16[160,2560]{1,0:T(8,128)(2,1)S(1)}, bf16[160,2560]{1,0:T(8,128)(2,1)S(1)}, u32[]{:S(2)}, u32[]{:S(2)}) collective-permute-start(bf16[160,2560]{1,0:T(8,128)(2,1)S(1)} %get-tuple-element.56.refs_0_.refs_4_), channel_id=1, source_target_pairs={{0,4},{1,5},{2,6},{3,7},{4,16},{5,17},{6,18},{7,19},{8,28},{9,29},... | collective-permute-start | bytes 2457608 | tf_op jit(solution)/shard_map/ppermute | solution.py:42
  45.5 10.4 %collective-permute-start.15 = (bf16[160,320]{1,0:T(8,128)(2,1)S(1)}, bf16[160,320]{1,0:T(8,128)(2,1)S(1)}, u32[]{:S(2)}, u32[]{:S(2)}) collective-permute-start(bf16[160,320]{1,0:T(8,128)(2,1)S(1)} %get-tuple-element.64.refs_4_.refs_0_), channel_id=1, source_target_pairs={{0,2},{1,3},{2,0},{3,1},{4,6},{5,7},{6,4},{7,5},{8,10},{9,11},{10,... | collective-permute-start | bytes 307208 | tf_op jit(solution)/shard_map/ppermute | solution.py:42
  47.7 8.3 %collective-permute-start.14 = (bf16[160,320]{1,0:T(8,128)(2,1)S(1)}, bf16[160,320]{1,0:T(8,128)(2,1)S(1)}, u32[]{:S(2)}, u32[]{:S(2)}) collective-permute-start(bf16[160,320]{1,0:T(8,128)(2,1)S(1)} %get-tuple-element.64.refs_4_.refs_0_), channel_id=1, source_target_pairs={{0,3},{1,0},{2,1},{3,2},{4,7},{5,4},{6,5},{7,6},{8,11},{9,8},{10,9... | collective-permute-start | bytes 307208 | tf_op jit(solution)/shard_map/ppermute | solution.py:42
  48.1 7.8 %collective-permute-start.13 = (bf16[160,320]{1,0:T(8,128)(2,1)S(1)}, bf16[160,320]{1,0:T(8,128)(2,1)S(1)}, u32[]{:S(2)}, u32[]{:S(2)}) collective-permute-start(bf16[160,320]{1,0:T(8,128)(2,1)S(1)} %get-tuple-element.64.refs_4_.refs_0_), channel_id=1, source_target_pairs={{0,1},{1,2},{2,3},{3,0},{4,5},{5,6},{6,7},{7,4},{8,9},{9,10},{10,1... | collective-permute-start | bytes 307208 | tf_op jit(solution)/shard_map/ppermute | solution.py:42
  55.9 7.8 %copy-start.2 = (bf16[256,256]{1,0:T(8,128)(2,1)S(1)}, bf16[256,256]{1,0:T(8,128)(2,1)}, u32[]{:S(2)}) copy-start(bf16[256,256]{1,0:T(8,128)(2,1)} %constant.17.clone.refs_3_) | copy-start | bytes 393220
  56.6 7.1 %collective-permute-start.18 = (bf16[160,2560]{1,0:T(8,128)(2,1)S(1)}, bf16[160,2560]{1,0:T(8,128)(2,1)S(1)}, u32[]{:S(2)}, u32[]{:S(2)}) collective-permute-start(bf16[160,2560]{1,0:T(8,128)(2,1)S(1)} %get-tuple-element.78.refs_6_), channel_id=1, source_target_pairs={{0,8},{1,9},{2,10},{3,11},{4,12},{5,13},{6,14},{7,15},{8,0},{9,1},... | collective-permute-start | bytes 2457608 | tf_op jit(solution)/shard_map/ppermute | solution.py:42
  58.7 2.7 %collective-permute-start.16 = (bf16[640,320]{1,0:T(8,128)(2,1)S(1)}, bf16[640,320]{1,0:T(8,128)(2,1)S(1)}, u32[]{:S(2)}, u32[]{:S(2)}) collective-permute-start(bf16[640,320]{1,0:T(8,128)(2,1)S(1)} %get-tuple-element.73.refs_2_), channel_id=1, source_target_pairs={{0,8},{1,9},{2,10},{3,11},{4,12},{5,13},{6,14},{7,15},{8,0},{9,1},... | collective-permute-start | bytes 1228808 | tf_op jit(solution)/shard_map/ppermute | solution.py:42
  58.8 9.4 %collective-permute-start.21 = (bf16[80,2560]{1,0:T(8,128)(2,1)S(1)}, bf16[80,2560]{1,0:T(8,128)(2,1)S(1)}, u32[]{:S(2)}, u32[]{:S(2)}) collective-permute-start(bf16[80,2560]{1,0:T(8,128)(2,1)S(1)} %slice.7), channel_id=1, source_target_pairs={{0,1},{1,2},{2,3},{3,0},{4,5},{5,6},{6,7},{7,4},{8,11},{9,8},{10,9... | collective-permute-start | bytes 1228808 | tf_op jit(solution)/shard_map/ppermute | solution.py:42
  60.4 7.8 %collective-permute-start.20 = (bf16[80,2560]{1,0:T(8,128)(2,1)S(1)}, bf16[80,2560]{1,0:T(8,128)(2,1)S(1)}, u32[]{:S(2)}, u32[]{:S(2)}) collective-permute-start(bf16[80,2560]{1,0:T(8,128)(2,1)S(1)} %slice.6), channel_id=1, source_target_pairs={{0,4},{1,5},{2,6},{3,7},{4,16},{5,17},{6,18},{7,19},{8,28},{9,29},... | collective-permute-start | bytes 1228808 | tf_op jit(solution)/shard_map/ppermute | solution.py:42
  60.8 2.9 %collective-permute-start.19 = (f32[80,320]{1,0:T(8,128)S(1)}, f32[80,320]{1,0:T(8,128)S(1)}, u32[]{:S(2)}, u32[]{:S(2)}) collective-permute-start(f32[80,320]{1,0:T(8,128)S(1)} %get-tuple-element.76.refs_4_.refs_0_), channel_id=1, source_target_pairs={{0,8},{1,9},{2,10},{3,11},{4,12},{5,13},{6,14},{7,15},{8,0},{9,1},... | collective-permute-start | bytes 307208 | tf_op jit(solution)/shard_map/ppermute | solution.py:42
  68.3 3.2 %collective-permute-start.22 = (bf16[160,2560]{1,0:T(8,128)(2,1)S(1)}, bf16[160,2560]{1,0:T(8,128)(2,1)S(1)}, u32[]{:S(2)}, u32[]{:S(2)}) collective-permute-start(bf16[160,2560]{1,0:T(8,128)(2,1)S(1)} %get-tuple-element.82), channel_id=1, source_target_pairs={{0,8},{1,9},{2,10},{3,11},{4,12},{5,13},{6,14},{7,15},{8,0},{9,1},... | collective-permute-start | bytes 2457608 | tf_op jit(solution)/shard_map/ppermute | solution.py:42

commit v3 on v2

--- a/solution.py
+++ b/solution.py
@@ -255,7 +255,9 @@
 
 def update_kernel(mine_ref, theirs_ref, left_ref, right_ref, out_ref):
     is_first = core_of() == 0
-    mine, theirs = mine_ref[...] / N_REP, theirs_ref[...] / N_REP
+    start = pl.multiple_of(lax.axis_index("fsdp") // 4 * TILE_ROWS, 16)
+    rows = pl.ds(start, TILE_ROWS)
+    mine, theirs = (ref[rows].astype(f32) / N_REP for ref in (mine_ref, theirs_ref))
     first = jnp.where(is_first, mine, theirs)
     second = jnp.where(is_first, theirs, mine)
     full = jnp.concatenate([first, second], axis=1)
@@ -278,7 +280,7 @@
 SIDES = (3, 0, 1, 2)
 
 
-def input_band_kernel(x_ref, pair_ref, high_ref, low_ref, turned_ref, held, pair, sems):
+def input_band_kernel(x_ref, pair_ref, band_ref, turned_ref, held, pair, sems):
     def copy(j):
         columns = pl.ds(j * WIDE, WIDE)
         return pltpu.make_async_copy(x_ref.at[0, :, columns], held.at[:, columns], sems.at[j])
@@ -292,7 +294,7 @@
         copy(j).wait()
         both = dot(held[:, j * WIDE : (j + 1) * WIDE], pair[...])
         bands = slice(j * NARROW, (j + 1) * NARROW)
-        high_ref[:, bands], low_ref[:, bands] = split(both[:, :NARROW] + both[:, NARROW:])
+        band_ref[:, bands] = (both[:, :NARROW] + both[:, NARROW:]).astype(bf16)
     shard = lax.axis_index("fsdp")
     here, z = shard // 4, lax.rem(shard, 4)
     wide = COLS // 2
@@ -313,7 +315,7 @@
     return call(
         input_band_kernel,
         [(inputs, ANY), (table["right_pair"], ANY)],
-        [part, part, ((TOKENS, COLS), bf16, VMEM)],
+        [part, ((TOKENS, COLS), bf16, VMEM)],
         scratch=[
             pltpu.VMEM((TOKENS, COLS), bf16),
             pltpu.VMEM((WIDE, 2 * NARROW), bf16),
@@ -341,10 +343,9 @@
     )
 
 
-def pair_kernel(own_ref, opposite_ref, left_ref, right_ref, own_out, pair_ref):
+def pair_kernel(own_ref, opposite_ref, left_ref, right_ref, pair_ref):
     own = own_ref[...] + opposite_ref[...]
     other = left_ref[...] + right_ref[...]
-    own_out[...] = own
     is_first = lax.axis_index("fsdp") < 4
     pair_ref[:TILE_ROWS] = jnp.where(is_first, own, other).astype(bf16)
     pair_ref[TILE_ROWS:] = jnp.where(is_first, other, own).astype(bf16)
@@ -354,7 +355,7 @@
     return call(
         pair_kernel,
         [(part, VMEM) for part in (own, opposite, left, right)],
-        [((TILE_ROWS, HALF), f32, VMEM), ((2 * TILE_ROWS, HALF), bf16, VMEM)],
+        [((2 * TILE_ROWS, HALF), bf16, VMEM)],
         name="pair",
         **order,
     )
@@ -386,7 +387,7 @@
     return call(hand_on_kernel, [], [], name=name, after=after, through=arrays)[1:]
 
 
-def change_kernel(high_ref, low_ref, bands_ref, s_bands_ref, out_ref, total):
+def change_kernel(high_ref, bands_ref, s_bands_ref, out_ref, total):
     core = core_of()
     z = lax.rem(lax.axis_index("fsdp"), 4)
     for k, side in enumerate((0, 3, 1, 2)):
@@ -397,17 +398,17 @@
             total[core, pl.ds(row, TILE_ROWS)] = bands_ref[rows]
             total[1 - core, pl.ds(row, TILE_ROWS)] = s_bands_ref[rows]
     for half in range(2):
-        value = dot(high_ref[...], total[half]) + dot(low_ref[...], total[half])
+        value = dot(high_ref[...], total[half])
         for k in range(5):
             high, low = split(value[:, k * 64 : (k + 1) * 64])
             start = (half * 5 + k) * 256
             out_ref[:, start : start + 256] = jnp.concatenate([high, low, high, low], axis=1)
 
 
-def change_of(high, low, bands, s_bands, **order):
+def change_of(high, bands, s_bands, **order):
     return call(
         change_kernel,
-        [(array, VMEM) for array in (high, low, bands, s_bands)],
+        [(array, VMEM) for array in (high, bands, s_bands)],
         [((TOKENS, COLS), bf16, VMEM)],
         scratch=[pltpu.VMEM((2, BANDS, HALF), bf16)],
         name="change",
@@ -549,7 +550,7 @@
     z1 = along_z(second)
     chip, _ = sum_of([mine, across(theirs)], "chip_sum")
     half_y = swapped(chip, 1, 0)
-    high, low, turned, done = input_band(inputs, table, after=[chip])
+    high, turned, done = input_band(inputs, table, after=[chip])
     half_sum, _, z0, x0 = sum_of(
         [chip, half_y], "half_y_sum", after=[done], through=[z0, x0]
     )
@@ -560,7 +561,7 @@
     column, _, z1, sz0 = sum_of([half_sum, rest_y], "y_sum", through=[z1, sz0])
     x_parts = by(column, 0, 2), by(column, 0, 1), by(column, 0, -1)
     new_momentum, done = momentum_less_band(moment, coeffs, table, after=[column])
-    own, pair, _, xz0, z2 = pair_of(column, *x_parts, after=[done], through=[xz0, z2])
+    pair, _, xz0, z2 = pair_of(column, *x_parts, after=[done], through=[xz0, z2])
     z_parts = by(pair, 2, 1), by(pair, 2, -1), by(pair, 2, 2)
     xz1 = along_x(z1)
     near, done = pack([z1, z2, xz0, x0], "pack_near", after=[pair])
@@ -572,15 +573,15 @@
     s_bands = across(bands)
     xz2 = along_x(z2[:QUARTER])
     z3 = along_z(xz0[QUARTER:])
-    xz1, own = hand_on([xz1, own], [done], "after_pack_bands")
-    sxz1, s_own = across(xz1), across(own)
-    change, done = change_of(high, low, bands, s_bands, after=[own])
-    acc, done, s_own = near_product(
-        turned, acc, change, [x0, xz0, xz1, s_near, sxz1], table, after=[done], through=[s_own]
+    xz1, s_bands = hand_on([xz1, s_bands], [done], "after_pack_bands")
+    sxz1 = across(xz1)
+    change, done = change_of(high, bands, s_bands)
+    acc, done = near_product(
+        turned, acc, change, [x0, xz0, xz1, s_near, sxz1], table, after=[done]
     )
     last, done = pack([xz2, z3], "pack_last", after=[done])
     s_last = across(last)
-    update, done = update_of(own, s_own, table, after=[done])
+    update, done = update_of(bands, s_bands, table, after=[done])
     result, update, _ = far_product(turned, acc, [xz2, z3, s_last], update, after=[done])
     return (new_momentum, update, result)
 

time: 75.3 us -> 75.2 us (level)
  waiting for transfers between devices: 12.9 us -> 13.8 us
  Pallas kernels: 31.9 us -> 31.1 us
    ppermute x21 -> x20, waiting for transfers between devices: 11.5 us -> 12.4 us  [moved(): return lax.ppermute(value, BOTH, pairs)]
    pallas_call x16, Pallas kernels: 31.9 us -> 31.1 us  [call(): pl.pallas_call(body, grid=grid, out_shape=tuple((pltpu.VMEM(shape, dtype)...]
    ppermute x21 -> x20, starting transfers between devices: 25.2 us -> 25.2 us  [moved(): return lax.ppermute(value, BOTH, pairs)]
  transfers between devices with their start and end apart: 23 -> 22, of which waited for: 10 -> 10; matrix products, arithmetic and copies ran while one was open for 0% -> 0% of each run, Pallas kernels for 30% -> 28%
where the time goes in v3:
time: 75.2 us; the launch traced here: 75.1 us
  Pallas kernels  31.1 us (41%)
  starting transfers between devices  29.2 us (39%)
  waiting for transfers between devices  13.8 us (18%)
  between operations  0.98 us (1%)
    pallas_call x16, Pallas kernels, call(): pl.pallas_call(body, grid=grid, out_shape=tuple((pltpu.VMEM(shape, dtype)...  31.1 us
    ppermute x20, starting transfers between devices, moved(): return lax.ppermute(value, BOTH, pairs)  25.2 us
    ppermute x20, waiting for transfers between devices, moved(): return lax.ppermute(value, BOTH, pairs)  12.4 us
    ppermute x2, starting transfers between devices, swapped(): return lax.ppermute(value, BOTH, pairs)  4.03 us
  transfers between devices with their start and end apart: 22, of which 10 were waited for; matrix products, arithmetic and copies ran while one was open for 0% of the time, Pallas kernels for 28%

profile of v3, /device:TPU:1, one launch (start us, length us, event | category | flops | bytes accessed | tf_op | source)
XLA Modules:
  0.0 75.1 jit_solution(16210357196247859764)
XLA Ops:
  0.6 4.8 %band.1 = (f32[80,640]{1,0:T(8,128)S(1)}, f32[80,320]{1,0:T(8,128)S(1)}, f32[80,320]{1,0:T(8,128)S(1)}, f32[320,2560]{1,0:T(8,128)S(1)}, bf16[160,2560]{1,0:T(8,...) custom-call(f32[1,320,2560]{2,1,0:T(8,128)} %refs_0_.2, bf16[1,320,2560]{2,1,0:T(8,128)(2,1)} %refs_1_.3, ...), custom_call_target="tpu_custom_call" | custom-call | flops 1 | bytes 1 | tf_op jit(solution)/shard_map/band/pallas_call | solution.py:125
  5.4 3.4 %collective-permute-start.3 = (bf16[160,2560]{1,0:T(8,128)(2,1)S(1)}, bf16[160,2560]{1,0:T(8,128)(2,1)S(1)}, u32[]{:S(2)}, u32[]{:S(2)}) collective-permute-start(bf16[160,2560]{1,0:T(8,128)(2,1)S(1)} %get-tuple-element.48), channel_id=1, source_target_pairs={{0,4},{1,5},{2,6},{3,7},{4,16},{5,17},{6,18},{7,19},{8,28},{9,29},... | collective-permute-start | bytes 2457608 | tf_op jit(solution)/shard_map/ppermute | solution.py:42
  8.8 3.8 %collective-permute-start.2 = (bf16[160,2560]{1,0:T(8,128)(2,1)S(1)}, bf16[160,2560]{1,0:T(8,128)(2,1)S(1)}, u32[]{:S(2)}, u32[]{:S(2)}) collective-permute-start(bf16[160,2560]{1,0:T(8,128)(2,1)S(1)} %get-tuple-element.48), channel_id=1, source_target_pairs={{0,1},{1,2},{2,3},{3,0},{4,5},{5,6},{6,7},{7,4},{8,11},{9,8},{10,9... | collective-permute-start | bytes 2457608 | tf_op jit(solution)/shard_map/ppermute | solution.py:42
  12.6 0.0 collective-permute-start
  12.6 1.3 %collective-permute-done.refs_1_ = f32[80,320]{1,0:T(8,128)S(1)} collective-permute-done((f32[80,320]{1,0:T(8,128)S(1)}, f32[80,320]{1,0:T(8,128)S(1)}, u32[]{:S(2)}, u32[]{:S(2)}) %collective-permute-start) | collective-permute-done | bytes 102432 | tf_op jit(solution)/shard_map/ppermute | solution.py:42
  13.9 0.6 chip_sum.1
  14.5 1.3 %collective-permute-start.1 = (f32[80,320]{1,0:T(8,128)S(1)}, f32[80,320]{1,0:T(8,128)S(1)}, u32[]{:S(2)}, u32[]{:S(2)}) collective-permute-start(f32[80,320]{1,0:T(8,128)S(1)} %get-tuple-element.45.refs_2_.refs_0_), channel_id=1, source_target_pairs={{0,32},{1,33},{2,34},{3,35},{4,36},{5,37},{6,38},{7,39},{8,40},{9,... | collective-permute-start | bytes 307208 | tf_op jit(solution)/shard_map/ppermute | solution.py:532
  15.8 0.0 copy-start
  15.8 0.1 collective-permute-start.5
  15.9 4.5 %input_band.1 = (bf16[640,640]{1,0:T(8,128)(2,1)S(1)}, bf16[640,2560]{1,0:T(8,128)(2,1)S(1)}, f32[8,128]{1,0:T(8,128)S(1)}) custom-call(bf16[1,640,2560]{2,1,0:T(8,128)(2,1)} %refs_0_.3, bf16[512,256]{1,0:T(8,128)(2,1)} %constant.14.clone.refs_1_, f32[80,320]{1,0:T(8,128)S(1)} %get-tuple-element.45.refs_2_.refs_0_), custom_call_target="tpu_custom_call" | custom-call | flops 1 | bytes 1 | tf_op jit(solution)/shard_map/input_band/pallas_call | solution.py:125
  20.5 0.0 collective-permute-done.1.refs_1_
  20.5 0.0 collective-permute-done.3.refs_4_
  20.5 1.4 %collective-permute-done.2.refs_3_ = bf16[160,2560]{1,0:T(8,128)(2,1)S(1)} collective-permute-done((bf16[160,2560]{1,0:T(8,128)(2,1)S(1)}, bf16[160,2560]{1,0:T(8,128)(2,1)S(1)}, u32[]{:S(2)}, u32[]{:S(2)}) %collective-permute-start.2) | collective-permute-done | bytes 819232 | tf_op jit(solution)/shard_map/ppermute | solution.py:42
  21.9 0.6 half_y_sum.1
  22.5 1.0 %collective-permute-start.6 = (bf16[160,2560]{1,0:T(8,128)(2,1)S(1)}, bf16[160,2560]{1,0:T(8,128)(2,1)S(1)}, u32[]{:S(2)}, u32[]{:S(2)}) collective-permute-start(bf16[160,2560]{1,0:T(8,128)(2,1)S(1)} %get-tuple-element.49.refs_2_), channel_id=1, source_target_pairs={{0,8},{1,9},{2,10},{3,11},{4,12},{5,13},{6,14},{7,15},{8,0},{9,1},... | collective-permute-start | bytes 2457608 | tf_op jit(solution)/shard_map/ppermute | solution.py:42
  23.5 2.1 %collective-permute-start.11 = (bf16[160,2560]{1,0:T(8,128)(2,1)S(1)}, bf16[160,2560]{1,0:T(8,128)(2,1)S(1)}, u32[]{:S(2)}, u32[]{:S(2)}) collective-permute-start(bf16[160,2560]{1,0:T(8,128)(2,1)S(1)} %get-tuple-element.49.refs_2_), channel_id=1, source_target_pairs={{0,1},{1,2},{2,3},{3,0},{4,5},{5,6},{6,7},{7,4},{8,11},{9,8},{10,9... | collective-permute-start | bytes 2457608 | tf_op jit(solution)/shard_map/ppermute | solution.py:42
  25.6 1.1 %collective-permute-start.10 = (bf16[160,2560]{1,0:T(8,128)(2,1)S(1)}, bf16[160,2560]{1,0:T(8,128)(2,1)S(1)}, u32[]{:S(2)}, u32[]{:S(2)}) collective-permute-start(bf16[160,2560]{1,0:T(8,128)(2,1)S(1)} %get-tuple-element.49.refs_2_), channel_id=1, source_target_pairs={{0,4},{1,5},{2,6},{3,7},{4,16},{5,17},{6,18},{7,19},{8,28},{9,29},... | collective-permute-start | bytes 2457608 | tf_op jit(solution)/shard_map/ppermute | solution.py:42
  26.7 2.7 %collective-permute-start.4 = (f32[80,320]{1,0:T(8,128)S(1)}, f32[80,320]{1,0:T(8,128)S(1)}, u32[]{:S(2)}, u32[]{:S(2)}) collective-permute-start(f32[80,320]{1,0:T(8,128)S(1)} %get-tuple-element.50.refs_0_), channel_id=1, source_target_pairs={{0,96},{1,97},{2,98},{3,99},{4,100},{5,101},{6,102},{7,103},{8,104... | collective-permute-start | bytes 307208 | tf_op jit(solution)/shard_map/ppermute | solution.py:532
  29.4 1.2 %collective-permute-done.5.refs_2_ = bf16[160,2560]{1,0:T(8,128)(2,1)S(1)} collective-permute-done((bf16[160,2560]{1,0:T(8,128)(2,1)S(1)}, bf16[160,2560]{1,0:T(8,128)(2,1)S(1)}, u32[]{:S(2)}, u32[]{:S(2)}) %collective-permute-start.5) | collective-permute-done | bytes 819232 | tf_op jit(solution)/shard_map/ppermute | solution.py:42
  30.6 1.3 %collective-permute-done.4.refs_1_ = f32[80,320]{1,0:T(8,128)S(1)} collective-permute-done((f32[80,320]{1,0:T(8,128)S(1)}, f32[80,320]{1,0:T(8,128)S(1)}, u32[]{:S(2)}, u32[]{:S(2)}) %collective-permute-start.4) | collective-permute-done | bytes 102432 | tf_op jit(solution)/shard_map/ppermute | solution.py:532
  32.0 0.0 collective-permute-done.6.refs_3_
  32.0 0.6 y_sum.1
  32.6 1.5 %collective-permute-start.9 = (f32[80,320]{1,0:T(8,128)S(1)}, f32[80,320]{1,0:T(8,128)S(1)}, u32[]{:S(2)}, u32[]{:S(2)}) collective-permute-start(f32[80,320]{1,0:T(8,128)S(1)} %get-tuple-element.54.refs_4_.refs_0_), channel_id=1, source_target_pairs={{0,20},{1,21},{2,22},{3,23},{4,0},{5,1},{6,2},{7,3},{8,28},{9,29},... | collective-permute-start | bytes 307208 | tf_op jit(solution)/shard_map/ppermute | solution.py:42
  34.1 0.0 collective-permute-start.8
  34.1 1.5 %collective-permute-start.7 = (f32[80,320]{1,0:T(8,128)S(1)}, f32[80,320]{1,0:T(8,128)S(1)}, u32[]{:S(2)}, u32[]{:S(2)}) collective-permute-start(f32[80,320]{1,0:T(8,128)S(1)} %get-tuple-element.54.refs_4_.refs_0_), channel_id=1, source_target_pairs={{0,16},{1,17},{2,18},{3,19},{4,20},{5,21},{6,22},{7,23},{8,24},{9,... | collective-permute-start | bytes 307208 | tf_op jit(solution)/shard_map/ppermute | solution.py:42
  35.6 0.0 copy-done
  35.6 0.0 copy-done.1
  35.6 1.6 %momentum_less_band.1 = (f32[1,320,2560]{2,1,0:T(8,128)S(1)}, f32[8,128]{1,0:T(8,128)S(1)}) custom-call(f32[320,2560]{1,0:T(8,128)S(1)} %get-tuple-element.55.refs_0_, f32[80,640]{1,0:T(8,128)S(1)} %get-tuple-element.56.refs_1_, bf16[320,240]{1,0:T(8,128)(2,1)S(1)} %copy-done.1, bf16[384,512]{1,0:T(8,128)(2,1)S(1)} %copy-done, ...), custom_call_target="tpu_custom_call" | custom-call | flops 1 | bytes 1 | tf_op jit(solution)/shard_map/momentum_less_band/pallas_call | solution.py:125
  37.2 2.2 %collective-permute-done.11.refs_6_ = bf16[160,2560]{1,0:T(8,128)(2,1)S(1)} collective-permute-done((bf16[160,2560]{1,0:T(8,128)(2,1)S(1)}, bf16[160,2560]{1,0:T(8,128)(2,1)S(1)}, u32[]{:S(2)}, u32[]{:S(2)}) %collective-permute-start.11) | collective-permute-done | bytes 819232 | tf_op jit(solution)/shard_map/ppermute | solution.py:42
  39.4 0.0 collective-permute-done.10.refs_5_
  39.4 0.7 collective-permute-done.9.refs_3_
  40.1 2.8 %collective-permute-done.8.refs_2_ = f32[80,320]{1,0:T(8,128)S(1)} collective-permute-done((f32[80,320]{1,0:T(8,128)S(1)}, f32[80,320]{1,0:T(8,128)S(1)}, u32[]{:S(2)}, u32[]{:S(2)}) %collective-permute-start.8) | collective-permute-done | bytes 102432 | tf_op jit(solution)/shard_map/ppermute | solution.py:42
  42.9 0.0 collective-permute-done.7.refs_1_
  42.9 0.6 pair.1
  43.6 0.2 pack_near.1
  43.8 0.8 %collective-permute-start.12 = (bf16[640,2560]{1,0:T(8,128)(2,1)S(1)}, bf16[640,2560]{1,0:T(8,128)(2,1)S(1)}, u32[]{:S(2)}, u32[]{:S(2)}) collective-permute-start(bf16[640,2560]{1,0:T(8,128)(2,1)S(1)} %get-tuple-element.62), channel_id=1, source_target_pairs={{0,8},{1,9},{2,10},{3,11},{4,12},{5,13},{6,14},{7,15},{8,0},{9,1},... | collective-permute-start | bytes 9830408 | tf_op jit(solution)/shard_map/ppermute | solution.py:42
  44.6 1.0 %collective-permute-start.16 = (bf16[160,2560]{1,0:T(8,128)(2,1)S(1)}, bf16[160,2560]{1,0:T(8,128)(2,1)S(1)}, u32[]{:S(2)}, u32[]{:S(2)}) collective-permute-start(bf16[160,2560]{1,0:T(8,128)(2,1)S(1)} %get-tuple-element.53.refs_0_.refs_4_), channel_id=1, source_target_pairs={{0,4},{1,5},{2,6},{3,7},{4,16},{5,17},{6,18},{7,19},{8,28},{9,29},... | collective-permute-start | bytes 2457608 | tf_op jit(solution)/shard_map/ppermute | solution.py:42
  45.6 2.1 %collective-permute-start.15 = (bf16[160,320]{1,0:T(8,128)(2,1)S(1)}, bf16[160,320]{1,0:T(8,128)(2,1)S(1)}, u32[]{:S(2)}, u32[]{:S(2)}) collective-permute-start(bf16[160,320]{1,0:T(8,128)(2,1)S(1)} %get-tuple-element.61.refs_4_.refs_0_), channel_id=1, source_target_pairs={{0,2},{1,3},{2,0},{3,1},{4,6},{5,7},{6,4},{7,5},{8,10},{9,11},{10,... | collective-permute-start | bytes 307208 | tf_op jit(solution)/shard_map/ppermute | solution.py:42
  47.8 0.5 collective-permute-start.14
  48.2 1.0 %collective-permute-start.13 = (bf16[160,320]{1,0:T(8,128)(2,1)S(1)}, bf16[160,320]{1,0:T(8,128)(2,1)S(1)}, u32[]{:S(2)}, u32[]{:S(2)}) collective-permute-start(bf16[160,320]{1,0:T(8,128)(2,1)S(1)} %get-tuple-element.61.refs_4_.refs_0_), channel_id=1, source_target_pairs={{0,1},{1,2},{2,3},{3,0},{4,5},{5,6},{6,7},{7,4},{8,9},{9,10},{10,1... | collective-permute-start | bytes 307208 | tf_op jit(solution)/shard_map/ppermute | solution.py:42
  49.2 0.8 %collective-permute-done.12.refs_6_.refs_7_ = bf16[640,2560]{1,0:T(8,128)(2,1)S(1)} collective-permute-done((bf16[640,2560]{1,0:T(8,128)(2,1)S(1)}, bf16[640,2560]{1,0:T(8,128)(2,1)S(1)}, u32[]{:S(2)}, u32[]{:S(2)}) %collective-permute-start.12) | collective-permute-done | bytes 3276832 | tf_op jit(solution)/shard_map/ppermute | solution.py:42
  50.1 5.9 %own_product.1 = (f32[640,2560]{1,0:T(8,128)S(1)}, f32[1,320,2560]{2,1,0:T(8,128)}, f32[8,128]{1,0:T(8,128)S(1)}) custom-call(bf16[640,2560]{1,0:T(8,128)(2,1)S(1)} %get-tuple-element.46.refs_0_, bf16[320,2560]{1,0:T(8,128)(2,1)} %refs_1_.4, bf16[160,2560]{1,0:T(8,128)(2,1)S(1)} %get-tuple-element.49.refs_2_, ...), custom_call_target="tpu_custom_call" | custom-call | flops 1 | bytes 1 | tf_op jit(solution)/shard_map/own_product/pallas_call | solution.py:125
  56.0 0.0 copy-start.2
  56.0 0.0 collective-permute-done.15.refs_3_
  56.0 0.0 collective-permute-done.14.refs_2_
  56.0 0.0 collective-permute-done.13.refs_1_
  56.1 0.5 collective-permute-start.17
  56.6 0.0 collective-permute-done.16.refs_1_
  56.6 1.5 %collective-permute-done.17.refs_2_ = bf16[640,320]{1,0:T(8,128)(2,1)S(1)} collective-permute-done((bf16[640,320]{1,0:T(8,128)(2,1)S(1)}, bf16[640,320]{1,0:T(8,128)(2,1)S(1)}, u32[]{:S(2)}, u32[]{:S(2)}) %collective-permute-start.17) | collective-permute-done | bytes 409632 | tf_op jit(solution)/shard_map/ppermute | solution.py:42
  58.0 0.6 after_pack_bands.1
  58.6 0.4 collective-permute-start.18
  59.1 1.6 %collective-permute-start.20 = (bf16[80,2560]{1,0:T(8,128)(2,1)S(1)}, bf16[80,2560]{1,0:T(8,128)(2,1)S(1)}, u32[]{:S(2)}, u32[]{:S(2)}) collective-permute-start(bf16[80,2560]{1,0:T(8,128)(2,1)S(1)} %slice.7), channel_id=1, source_target_pairs={{0,1},{1,2},{2,3},{3,0},{4,5},{5,6},{6,7},{7,4},{8,11},{9,8},{10,9... | collective-permute-start | bytes 1228808 | tf_op jit(solution)/shard_map/ppermute | solution.py:42
  60.7 2.1 %collective-permute-start.19 = (bf16[80,2560]{1,0:T(8,128)(2,1)S(1)}, bf16[80,2560]{1,0:T(8,128)(2,1)S(1)}, u32[]{:S(2)}, u32[]{:S(2)}) collective-permute-start(bf16[80,2560]{1,0:T(8,128)(2,1)S(1)} %slice.6), channel_id=1, source_target_pairs={{0,4},{1,5},{2,6},{3,7},{4,16},{5,17},{6,18},{7,19},{8,28},{9,29},... | collective-permute-start | bytes 1228808 | tf_op jit(solution)/shard_map/ppermute | solution.py:42
  62.8 1.3 %change.1 = (bf16[640,2560]{1,0:T(8,128)(2,1)S(1)}, f32[8,128]{1,0:T(8,128)S(1)}) custom-call(bf16[640,640]{1,0:T(8,128)(2,1)S(1)} %get-tuple-element.67.refs_0_, bf16[640,320]{1,0:T(8,128)(2,1)S(1)} %get-tuple-element.69.refs_1_.refs_0_, bf16[640,320]{1,0:T(8,128)(2,1)S(1)} %get-tuple-element.71.refs_2_.refs_1_), custom_call_target="tpu_custom_call" | custom-call | flops 1 | bytes 1 | tf_op jit(solution)/shard_map/change/pallas_call | solution.py:125
  64.2 0.0 collective-permute-done.18.refs_8_
  64.2 0.0 copy-done.2
  64.2 4.4 %near_product.1 = (f32[640,2560]{1,0:T(8,128)S(1)}, f32[8,128]{1,0:T(8,128)S(1)}) custom-call(bf16[640,2560]{1,0:T(8,128)(2,1)S(1)} %get-tuple-element.46.refs_0_, f32[640,2560]{1,0:T(8,128)S(1)} %get-tuple-element.66.refs_1_, bf16[640,2560]{1,0:T(8,128)(2,1)S(1)} %get-tuple-element.72.refs_2_, bf16[256,256]{1,0:T(8,128)(2,1)S(1)} %copy-done.2, ...), custom_call_target="tpu_custom_call" | custom-call | flops 1 | bytes 1 | tf_op jit(solution)/shard_map/near_product/pallas_call | solution.py:125
  68.6 0.0 collective-permute-done.20.refs_1_.refs_3_
  68.7 0.0 collective-permute-done.19.refs_0_.refs_2_
  68.7 0.1 pack_last.1
  68.7 0.7 collective-permute-start.21
  69.4 1.6 %update.1 = (f32[320,2560]{1,0:T(8,128)S(1)}, f32[8,128]{1,0:T(8,128)S(1)}) custom-call(bf16[640,320]{1,0:T(8,128)(2,1)S(1)} %get-tuple-element.69.refs_1_.refs_0_, bf16[640,320]{1,0:T(8,128)(2,1)S(1)} %get-tuple-element.71.refs_2_.refs_1_, bf16[320,240]{1,0:T(8,128)(2,1)S(1)} %copy-done.1, bf16[384,512]{1,0:T(8,128)(2,1)S(1)} %copy-done, ...), custom_call_target="tpu_custom_call" | custom-call | flops 1 | bytes 1 | tf_op jit(solution)/shard_map/update/pallas_call | solution.py:125
  71.0 0.4 collective-permute-done.21.refs_4_
  71.4 3.5 %far_product.1 = (bf16[1,640,2560]{2,1,0:T(8,128)(2,1)}, f32[320,2560]{1,0:T(8,128)}, f32[8,128]{1,0:T(8,128)}) custom-call(bf16[640,2560]{1,0:T(8,128)(2,1)S(1)} %get-tuple-element.46.refs_0_, f32[640,2560]{1,0:T(8,128)S(1)} %get-tuple-element.75.refs_1_, bf16[80,2560]{1,0:T(8,128)(2,1)S(1)} %collective-permute-done.19.refs_0_.refs_2_, ...), custom_call_target="tpu_custom_call" | custom-call | flops 1 | bytes 1 | tf_op jit(solution)/shard_map/far_product/pallas_call | solution.py:125
  (4 shorter events, 0.1 us)
Async XLA Ops:
  5.4 15.0 %collective-permute-start.3 = (bf16[160,2560]{1,0:T(8,128)(2,1)S(1)}, bf16[160,2560]{1,0:T(8,128)(2,1)S(1)}, u32[]{:S(2)}, u32[]{:S(2)}) collective-permute-start(bf16[160,2560]{1,0:T(8,128)(2,1)S(1)} %get-tuple-element.48), channel_id=1, source_target_pairs={{0,4},{1,5},{2,6},{3,7},{4,16},{5,17},{6,18},{7,19},{8,28},{9,29},... | collective-permute-start | bytes 2457608 | tf_op jit(solution)/shard_map/ppermute | solution.py:42
  8.8 13.0 %collective-permute-start.2 = (bf16[160,2560]{1,0:T(8,128)(2,1)S(1)}, bf16[160,2560]{1,0:T(8,128)(2,1)S(1)}, u32[]{:S(2)}, u32[]{:S(2)}) collective-permute-start(bf16[160,2560]{1,0:T(8,128)(2,1)S(1)} %get-tuple-element.48), channel_id=1, source_target_pairs={{0,1},{1,2},{2,3},{3,0},{4,5},{5,6},{6,7},{7,4},{8,11},{9,8},{10,9... | collective-permute-start | bytes 2457608 | tf_op jit(solution)/shard_map/ppermute | solution.py:42
  12.6 1.3 %collective-permute-start = (f32[80,320]{1,0:T(8,128)S(1)}, f32[80,320]{1,0:T(8,128)S(1)}, u32[]{:S(2)}, u32[]{:S(2)}) collective-permute-start(f32[80,320]{1,0:T(8,128)S(1)} %get-tuple-element.44), channel_id=1, source_target_pairs={{0,8},{1,9},{2,10},{3,11},{4,12},{5,13},{6,14},{7,15},{8,0},{9,1},... | collective-permute-start | bytes 307208 | tf_op jit(solution)/shard_map/ppermute | solution.py:42
  14.5 6.0 %collective-permute-start.1 = (f32[80,320]{1,0:T(8,128)S(1)}, f32[80,320]{1,0:T(8,128)S(1)}, u32[]{:S(2)}, u32[]{:S(2)}) collective-permute-start(f32[80,320]{1,0:T(8,128)S(1)} %get-tuple-element.45.refs_2_.refs_0_), channel_id=1, source_target_pairs={{0,32},{1,33},{2,34},{3,35},{4,36},{5,37},{6,38},{7,39},{8,40},{9,... | collective-permute-start | bytes 307208 | tf_op jit(solution)/shard_map/ppermute | solution.py:532
  15.8 19.8 %copy-start = (bf16[384,512]{1,0:T(8,128)(2,1)S(1)}, bf16[384,512]{1,0:T(8,128)(2,1)}, u32[]{:S(2)}) copy-start(bf16[384,512]{1,0:T(8,128)(2,1)} %constant.16.clone.refs_3_) | copy-start | bytes 1179652
  15.8 19.8 %copy-start.1 = (bf16[320,240]{1,0:T(8,128)(2,1)S(1)}, bf16[320,240]{1,0:T(8,128)(2,1)}, u32[]{:S(2)}) copy-start(bf16[320,240]{1,0:T(8,128)(2,1)} %constant.15.clone.refs_2_) | copy-start | bytes 460804
  15.8 14.8 %collective-permute-start.5 = (bf16[160,2560]{1,0:T(8,128)(2,1)S(1)}, bf16[160,2560]{1,0:T(8,128)(2,1)S(1)}, u32[]{:S(2)}, u32[]{:S(2)}) collective-permute-start(bf16[160,2560]{1,0:T(8,128)(2,1)S(1)} %get-tuple-element.51), channel_id=1, source_target_pairs={{0,1},{1,2},{2,3},{3,0},{4,5},{5,6},{6,7},{7,4},{8,11},{9,8},{10,9... | collective-permute-start | bytes 2457608 | tf_op jit(solution)/shard_map/ppermute | solution.py:42
  22.5 9.5 %collective-permute-start.6 = (bf16[160,2560]{1,0:T(8,128)(2,1)S(1)}, bf16[160,2560]{1,0:T(8,128)(2,1)S(1)}, u32[]{:S(2)}, u32[]{:S(2)}) collective-permute-start(bf16[160,2560]{1,0:T(8,128)(2,1)S(1)} %get-tuple-element.49.refs_2_), channel_id=1, source_target_pairs={{0,8},{1,9},{2,10},{3,11},{4,12},{5,13},{6,14},{7,15},{8,0},{9,1},... | collective-permute-start | bytes 2457608 | tf_op jit(solution)/shard_map/ppermute | solution.py:42
  23.5 15.9 %collective-permute-start.11 = (bf16[160,2560]{1,0:T(8,128)(2,1)S(1)}, bf16[160,2560]{1,0:T(8,128)(2,1)S(1)}, u32[]{:S(2)}, u32[]{:S(2)}) collective-permute-start(bf16[160,2560]{1,0:T(8,128)(2,1)S(1)} %get-tuple-element.49.refs_2_), channel_id=1, source_target_pairs={{0,1},{1,2},{2,3},{3,0},{4,5},{5,6},{6,7},{7,4},{8,11},{9,8},{10,9... | collective-permute-start | bytes 2457608 | tf_op jit(solution)/shard_map/ppermute | solution.py:42
  25.6 13.8 %collective-permute-start.10 = (bf16[160,2560]{1,0:T(8,128)(2,1)S(1)}, bf16[160,2560]{1,0:T(8,128)(2,1)S(1)}, u32[]{:S(2)}, u32[]{:S(2)}) collective-permute-start(bf16[160,2560]{1,0:T(8,128)(2,1)S(1)} %get-tuple-element.49.refs_2_), channel_id=1, source_target_pairs={{0,4},{1,5},{2,6},{3,7},{4,16},{5,17},{6,18},{7,19},{8,28},{9,29},... | collective-permute-start | bytes 2457608 | tf_op jit(solution)/shard_map/ppermute | solution.py:42
  26.7 5.3 %collective-permute-start.4 = (f32[80,320]{1,0:T(8,128)S(1)}, f32[80,320]{1,0:T(8,128)S(1)}, u32[]{:S(2)}, u32[]{:S(2)}) collective-permute-start(f32[80,320]{1,0:T(8,128)S(1)} %get-tuple-element.50.refs_0_), channel_id=1, source_target_pairs={{0,96},{1,97},{2,98},{3,99},{4,100},{5,101},{6,102},{7,103},{8,104... | collective-permute-start | bytes 307208 | tf_op jit(solution)/shard_map/ppermute | solution.py:532
  32.6 7.5 %collective-permute-start.9 = (f32[80,320]{1,0:T(8,128)S(1)}, f32[80,320]{1,0:T(8,128)S(1)}, u32[]{:S(2)}, u32[]{:S(2)}) collective-permute-start(f32[80,320]{1,0:T(8,128)S(1)} %get-tuple-element.54.refs_4_.refs_0_), channel_id=1, source_target_pairs={{0,20},{1,21},{2,22},{3,23},{4,0},{5,1},{6,2},{7,3},{8,28},{9,29},... | collective-permute-start | bytes 307208 | tf_op jit(solution)/shard_map/ppermute | solution.py:42
  34.1 8.9 %collective-permute-start.8 = (f32[80,320]{1,0:T(8,128)S(1)}, f32[80,320]{1,0:T(8,128)S(1)}, u32[]{:S(2)}, u32[]{:S(2)}) collective-permute-start(f32[80,320]{1,0:T(8,128)S(1)} %get-tuple-element.54.refs_4_.refs_0_), channel_id=1, source_target_pairs={{0,4},{1,5},{2,6},{3,7},{4,16},{5,17},{6,18},{7,19},{8,12},{9,13},... | collective-permute-start | bytes 307208 | tf_op jit(solution)/shard_map/ppermute | solution.py:42
  34.1 8.9 %collective-permute-start.7 = (f32[80,320]{1,0:T(8,128)S(1)}, f32[80,320]{1,0:T(8,128)S(1)}, u32[]{:S(2)}, u32[]{:S(2)}) collective-permute-start(f32[80,320]{1,0:T(8,128)S(1)} %get-tuple-element.54.refs_4_.refs_0_), channel_id=1, source_target_pairs={{0,16},{1,17},{2,18},{3,19},{4,20},{5,21},{6,22},{7,23},{8,24},{9,... | collective-permute-start | bytes 307208 | tf_op jit(solution)/shard_map/ppermute | solution.py:42
  43.8 6.3 %collective-permute-start.12 = (bf16[640,2560]{1,0:T(8,128)(2,1)S(1)}, bf16[640,2560]{1,0:T(8,128)(2,1)S(1)}, u32[]{:S(2)}, u32[]{:S(2)}) collective-permute-start(bf16[640,2560]{1,0:T(8,128)(2,1)S(1)} %get-tuple-element.62), channel_id=1, source_target_pairs={{0,8},{1,9},{2,10},{3,11},{4,12},{5,13},{6,14},{7,15},{8,0},{9,1},... | collective-permute-start | bytes 9830408 | tf_op jit(solution)/shard_map/ppermute | solution.py:42
  44.6 12.0 %collective-permute-start.16 = (bf16[160,2560]{1,0:T(8,128)(2,1)S(1)}, bf16[160,2560]{1,0:T(8,128)(2,1)S(1)}, u32[]{:S(2)}, u32[]{:S(2)}) collective-permute-start(bf16[160,2560]{1,0:T(8,128)(2,1)S(1)} %get-tuple-element.53.refs_0_.refs_4_), channel_id=1, source_target_pairs={{0,4},{1,5},{2,6},{3,7},{4,16},{5,17},{6,18},{7,19},{8,28},{9,29},... | collective-permute-start | bytes 2457608 | tf_op jit(solution)/shard_map/ppermute | solution.py:42
  45.6 10.4 %collective-permute-start.15 = (bf16[160,320]{1,0:T(8,128)(2,1)S(1)}, bf16[160,320]{1,0:T(8,128)(2,1)S(1)}, u32[]{:S(2)}, u32[]{:S(2)}) collective-permute-start(bf16[160,320]{1,0:T(8,128)(2,1)S(1)} %get-tuple-element.61.refs_4_.refs_0_), channel_id=1, source_target_pairs={{0,2},{1,3},{2,0},{3,1},{4,6},{5,7},{6,4},{7,5},{8,10},{9,11},{10,... | collective-permute-start | bytes 307208 | tf_op jit(solution)/shard_map/ppermute | solution.py:42
  47.8 8.3 %collective-permute-start.14 = (bf16[160,320]{1,0:T(8,128)(2,1)S(1)}, bf16[160,320]{1,0:T(8,128)(2,1)S(1)}, u32[]{:S(2)}, u32[]{:S(2)}) collective-permute-start(bf16[160,320]{1,0:T(8,128)(2,1)S(1)} %get-tuple-element.61.refs_4_.refs_0_), channel_id=1, source_target_pairs={{0,3},{1,0},{2,1},{3,2},{4,7},{5,4},{6,5},{7,6},{8,11},{9,8},{10,9... | collective-permute-start | bytes 307208 | tf_op jit(solution)/shard_map/ppermute | solution.py:42
  48.2 7.8 %collective-permute-start.13 = (bf16[160,320]{1,0:T(8,128)(2,1)S(1)}, bf16[160,320]{1,0:T(8,128)(2,1)S(1)}, u32[]{:S(2)}, u32[]{:S(2)}) collective-permute-start(bf16[160,320]{1,0:T(8,128)(2,1)S(1)} %get-tuple-element.61.refs_4_.refs_0_), channel_id=1, source_target_pairs={{0,1},{1,2},{2,3},{3,0},{4,5},{5,6},{6,7},{7,4},{8,9},{9,10},{10,1... | collective-permute-start | bytes 307208 | tf_op jit(solution)/shard_map/ppermute | solution.py:42
  56.0 8.2 %copy-start.2 = (bf16[256,256]{1,0:T(8,128)(2,1)S(1)}, bf16[256,256]{1,0:T(8,128)(2,1)}, u32[]{:S(2)}) copy-start(bf16[256,256]{1,0:T(8,128)(2,1)} %constant.17.clone.refs_3_) | copy-start | bytes 393220
  56.1 1.9 %collective-permute-start.17 = (bf16[640,320]{1,0:T(8,128)(2,1)S(1)}, bf16[640,320]{1,0:T(8,128)(2,1)S(1)}, u32[]{:S(2)}, u32[]{:S(2)}) collective-permute-start(bf16[640,320]{1,0:T(8,128)(2,1)S(1)} %get-tuple-element.69.refs_1_.refs_0_), channel_id=1, source_target_pairs={{0,8},{1,9},{2,10},{3,11},{4,12},{5,13},{6,14},{7,15},{8,0},{9,1},... | collective-permute-start | bytes 1228808 | tf_op jit(solution)/shard_map/ppermute | solution.py:42
  58.6 5.5 %collective-permute-start.18 = (bf16[160,2560]{1,0:T(8,128)(2,1)S(1)}, bf16[160,2560]{1,0:T(8,128)(2,1)S(1)}, u32[]{:S(2)}, u32[]{:S(2)}) collective-permute-start(bf16[160,2560]{1,0:T(8,128)(2,1)S(1)} %get-tuple-element.73.refs_6_), channel_id=1, source_target_pairs={{0,8},{1,9},{2,10},{3,11},{4,12},{5,13},{6,14},{7,15},{8,0},{9,1},... | collective-permute-start | bytes 2457608 | tf_op jit(solution)/shard_map/ppermute | solution.py:42
  59.1 9.6 %collective-permute-start.20 = (bf16[80,2560]{1,0:T(8,128)(2,1)S(1)}, bf16[80,2560]{1,0:T(8,128)(2,1)S(1)}, u32[]{:S(2)}, u32[]{:S(2)}) collective-permute-start(bf16[80,2560]{1,0:T(8,128)(2,1)S(1)} %slice.7), channel_id=1, source_target_pairs={{0,1},{1,2},{2,3},{3,0},{4,5},{5,6},{6,7},{7,4},{8,11},{9,8},{10,9... | collective-permute-start | bytes 1228808 | tf_op jit(solution)/shard_map/ppermute | solution.py:42
  60.7 7.9 %collective-permute-start.19 = (bf16[80,2560]{1,0:T(8,128)(2,1)S(1)}, bf16[80,2560]{1,0:T(8,128)(2,1)S(1)}, u32[]{:S(2)}, u32[]{:S(2)}) collective-permute-start(bf16[80,2560]{1,0:T(8,128)(2,1)S(1)} %slice.6), channel_id=1, source_target_pairs={{0,4},{1,5},{2,6},{3,7},{4,16},{5,17},{6,18},{7,19},{8,28},{9,29},... | collective-permute-start | bytes 1228808 | tf_op jit(solution)/shard_map/ppermute | solution.py:42
  68.7 2.7 %collective-permute-start.21 = (bf16[160,2560]{1,0:T(8,128)(2,1)S(1)}, bf16[160,2560]{1,0:T(8,128)(2,1)S(1)}, u32[]{:S(2)}, u32[]{:S(2)}) collective-permute-start(bf16[160,2560]{1,0:T(8,128)(2,1)S(1)} %get-tuple-element.77), channel_id=1, source_target_pairs={{0,8},{1,9},{2,10},{3,11},{4,12},{5,13},{6,14},{7,15},{8,0},{9,1},... | collective-permute-start | bytes 2457608 | tf_op jit(solution)/shard_map/ppermute | solution.py:42
